TPU v7x, 32 devices: a whole 2x2x4 slice. The times are simulated.
32 devices in a mesh: dp: 4 (over y, core), expert: 8 (over z, x).
Axes of the slice: x: 2, y: 2, z: 4, core: 2. Of those that a mesh axis runs over, the one named last changes fastest.
Arguments:
- tokens: bfloat16 [512, 3584], P('expert', 'dp'), may hold values from -6 to 6
- expert_ids: int32 [512, 8], P('expert'), may hold values from 0 to 31, as said below
- gate_weights: float32 [512, 8], P('expert'), may hold values from 0.1 to 1
- w_gate: bfloat16 [32, 3584, 1024], P('expert', 'dp'), may hold values from -0.09375 to 0.09375
- w_up: bfloat16 [32, 3584, 1024], P('expert', 'dp'), may hold values from -0.09375 to 0.09375
- w_down: bfloat16 [32, 1024, 3584], P('expert', None, 'dp'), may hold values from -0.1875 to 0.1875
- cotangent: bfloat16 [512, 3584], P('expert', 'dp'), may hold values from -6 to 6
Outputs:
- mixed: bfloat16 [512, 3584], P('expert', 'dp')
- token_grad: bfloat16 [512, 3584], P('expert', 'dp')
- grad_gate: bfloat16 [32, 3584, 1024], P('expert', 'dp')
- grad_up: bfloat16 [32, 3584, 1024], P('expert', 'dp')
- grad_down: bfloat16 [32, 1024, 3584], P('expert', None, 'dp')
Inputs may be any that keep to these rules, and one draw needn't show every extreme that they name: `expert_ids`: each row names 8 different experts. In each aligned block of 64 rows (the rows of one device) no expert is named by more than 32 rows, and one expert, the same in every block, is named by exactly 32 rows of every block.
All inputs are finite; a program needn't handle non-finite values.
Results may differ from a plain program's by a relative error of at most 0.035.
Values may be sent and summed in bfloat16 or wider, within the bound.
A program may use at most 128 MiB of HBM per device.

v0:
```python
import jax
import jax.numpy as jnp
from jax import lax
from jax.sharding import PartitionSpec as P

EXPERTS = 32
CAP = 32


def slot_table(expert_ids, gate_weights, first_expert, local_count):
    flat_ids = expert_ids.reshape(-1)
    numbers = jnp.arange(EXPERTS, dtype=jnp.int32)
    onehot = (flat_ids[:, None] == numbers[None, :]).astype(jnp.int32)
    slot_rank = jnp.sum((jnp.cumsum(onehot, axis=0) - 1) * onehot, axis=1)
    slot_number = (flat_ids - first_expert) * CAP + slot_rank
    inside = (flat_ids >= first_expert) & (flat_ids < first_expert + local_count)
    slot_list = jnp.arange(local_count * CAP, dtype=jnp.int32)
    matches = (slot_number[None, :] == slot_list[:, None]) & inside[None, :]
    matches = matches.reshape(local_count * CAP, expert_ids.shape[0], expert_ids.shape[1])
    pick_table = jnp.sum(matches, axis=2).astype(jnp.float32)
    weighted = jnp.sum(jnp.where(matches, gate_weights[None, :, :], 0.0), axis=2)
    return (pick_table, weighted)


def expert_pass(rows_in, rows_dy, w_gate, w_up, w_down):
    gate_part = jnp.einsum("erd,edf->erf", rows_in, w_gate, preferred_element_type=jnp.float32)
    up_part = jnp.einsum("erd,edf->erf", rows_in, w_up, preferred_element_type=jnp.float32)
    gate_sum, up_sum = (
        lax.psum(gate_part.astype(jnp.bfloat16), "dp").astype(jnp.float32),
        lax.psum(up_part.astype(jnp.bfloat16), "dp").astype(jnp.float32),
    )
    logistic = jax.nn.sigmoid(gate_sum)
    hidden = (gate_sum * logistic * up_sum).astype(jnp.bfloat16)
    out_rows = jnp.einsum(
        "erf,efd->erd", hidden, w_down, preferred_element_type=jnp.float32
    ).astype(jnp.bfloat16)
    grad_part = jnp.einsum("erd,efd->erf", rows_dy, w_down, preferred_element_type=jnp.float32)
    hidden_grad = lax.psum(grad_part.astype(jnp.bfloat16), "dp").astype(jnp.float32)
    up_grad = (hidden_grad * gate_sum * logistic).astype(jnp.bfloat16)
    gate_grad = (hidden_grad * up_sum * logistic * (1.0 + gate_sum * (1.0 - logistic))).astype(
        jnp.bfloat16
    )
    row_grad = (
        jnp.einsum("erf,edf->erd", gate_grad, w_gate, preferred_element_type=jnp.float32)
        + jnp.einsum("erf,edf->erd", up_grad, w_up, preferred_element_type=jnp.float32)
    ).astype(jnp.bfloat16)
    grad_gate = jnp.einsum(
        "erd,erf->edf", rows_in, gate_grad, preferred_element_type=jnp.float32
    ).astype(jnp.bfloat16)
    grad_up = jnp.einsum(
        "erd,erf->edf", rows_in, up_grad, preferred_element_type=jnp.float32
    ).astype(jnp.bfloat16)
    grad_down = jnp.einsum(
        "erf,erd->efd", hidden, rows_dy, preferred_element_type=jnp.float32
    ).astype(jnp.bfloat16)
    return (out_rows, row_grad, grad_gate, grad_up, grad_down)


def body(tokens, expert_ids, gate_weights, w_gate, w_up, w_down, cotangent):
    width = tokens.shape[1]
    pick_table, weighted = slot_table(expert_ids, gate_weights, 0, EXPERTS)
    send_in = jnp.dot(pick_table.astype(jnp.bfloat16), tokens, preferred_element_type=jnp.float32)
    send_in = send_in.astype(jnp.bfloat16).reshape(EXPERTS, CAP, width)
    send_dy = jnp.dot(weighted, cotangent.astype(jnp.float32), precision=lax.Precision.HIGHEST)
    send_dy = send_dy.astype(jnp.bfloat16).reshape(EXPERTS, CAP, width)
    rows_in, rows_dy = (
        lax.all_to_all(send_in, "expert", split_axis=0, concat_axis=1, tiled=True),
        lax.all_to_all(send_dy, "expert", split_axis=0, concat_axis=1, tiled=True),
    )
    out_rows, row_grad, grad_gate, grad_up, grad_down = expert_pass(
        rows_in, rows_dy, w_gate, w_up, w_down
    )
    back_out, back_grad = (
        lax.all_to_all(out_rows, "expert", split_axis=1, concat_axis=0, tiled=True),
        lax.all_to_all(row_grad, "expert", split_axis=1, concat_axis=0, tiled=True),
    )
    mixed = jnp.dot(
        weighted.T,
        back_out.reshape(EXPERTS * CAP, width).astype(jnp.float32),
        precision=lax.Precision.HIGHEST,
    )
    token_grad = jnp.dot(
        pick_table.T,
        back_grad.reshape(EXPERTS * CAP, width).astype(jnp.float32),
        precision=lax.Precision.HIGHEST,
    )
    return (
        mixed.astype(jnp.bfloat16),
        token_grad.astype(jnp.bfloat16),
        grad_gate,
        grad_up,
        grad_down,
    )


def solution(mesh):
    placed = (
        P("expert", "dp"),
        P("expert", None),
        P("expert", None),
        P("expert", "dp", None),
        P("expert", "dp", None),
        P("expert", None, "dp"),
        P("expert", "dp"),
    )
    return jax.shard_map(
        body,
        mesh=mesh,
        in_specs=placed,
        out_specs=(
            P("expert", "dp"),
            P("expert", "dp"),
            P("expert", "dp", None),
            P("expert", "dp", None),
            P("expert", None, "dp"),
        ),
        check_vma=False,
    )
```

profile of v0, /device:TPU:0, one launch (start us, length us, event | category | flops | bytes accessed | tf_op | source)
XLA Modules:
  0.0 361.4 jit_solution(18284925140923356536)
XLA Ops:
  9.0 1.2 reduce-window.6
  11.5 0.8 convert_reduce_fusion
  12.3 1.9 convolution_convert_fusion.7
  14.2 7.4 %all-to-all-start = ((bf16[32,32,896]{2,1,0:T(8,128)(2,1)}), bf16[32,32,896]{2,1,0:T(8,128)(2,1)S(1)}, u32[]{:S(2)}, u32[]{:S(2)}) async-start(bf16[32,32,896]{2,1,0:T(8,128)(2,1)} %bitcast.59), calls=%async_computation | async-start | bytes 3670016 | tf_op jit(solution)/shard_map/all_to_all | solution.py:67
  21.7 0.9 select_reduce_fusion
  22.6 2.9 convolution_convert_fusion.8
  25.4 38.7 %all-to-all-done = bf16[32,32,896]{2,1,0:T(8,128)(2,1)S(1)} async-done(((bf16[32,32,896]{2,1,0:T(8,128)(2,1)}), bf16[32,32,896]{2,1,0:T(8,128)(2,1)S(1)}, u32[]{:S(2)}, u32[]{:S(2)}) %all-to-all-start) | async-done | bytes 1835040 | tf_op jit(solution)/shard_map/all_to_all | solution.py:67
  64.2 4.3 %all-to-all-start.2 = ((bf16[32,32,896]{2,1,0:T(8,128)(2,1)}), bf16[32,32,896]{2,1,0:T(8,128)(2,1)}, u32[]{:S(2)}, u32[]{:S(2)}) async-start(bf16[32,32,896]{2,1,0:T(8,128)(2,1)} %bitcast.58), calls=%async_computation.2 | async-start | bytes 3670016 | tf_op jit(solution)/shard_map/all_to_all | solution.py:68
  68.8 1.5 copy.103
  70.3 40.5 %all-to-all-done.2 = bf16[32,32,896]{2,1,0:T(8,128)(2,1)} async-done(((bf16[32,32,896]{2,1,0:T(8,128)(2,1)}), bf16[32,32,896]{2,1,0:T(8,128)(2,1)}, u32[]{:S(2)}, u32[]{:S(2)}) %all-to-all-start.2) | async-done | bytes 1835040 | tf_op jit(solution)/shard_map/all_to_all | solution.py:68
  110.7 1.8 copy.107
  112.6 7.4 %convolution_convert_fusion.4 = bf16[4,256,1024]{2,1,0:T(8,128)(2,1)} fusion(bf16[4,256,896]{2,1,0:T(8,128)(2,1)S(1)} %bitcast.63, bf16[4,896,1024]{2,1,0:T(8,128)(2,1)} %param.11), kind=kOutput, calls=%fused_computation.25 | convolution fusion | flops 1880096768 | bytes 11272192 | tf_op jit(solution)/shard_map/erd,edf->erf/dot_general | solution.py:27
  120.1 3.8 %convolution_convert_fusion.5 = bf16[4,256,1024]{2,1,0:T(8,128)(2,1)} fusion(bf16[4,256,896]{2,1,0:T(8,128)(2,1)S(1)} %bitcast.64, bf16[4,896,1024]{2,1,0:T(8,128)(2,1)S(1)} %bitcast.54), kind=kOutput, calls=%fused_computation.26 | convolution fusion | flops 1880096768 | bytes 11272192 | tf_op jit(solution)/shard_map/erd,edf->erf/dot_general | solution.py:26
  123.8 3.7 %convolution_convert_fusion.3 = bf16[4,256,1024]{2,1,0:T(8,128)(2,1)} fusion(bf16[4,256,896]{2,1,0:T(8,128)(2,1)S(1)} %bitcast.66, bf16[4,1024,896]{2,1,0:T(8,128)(2,1)S(1)} %bitcast.69), kind=kOutput, calls=%fused_computation.24 | convolution fusion | flops 1880096768 | bytes 11272192 | tf_op jit(solution)/shard_map/erd,efd->erf/dot_general | solution.py:37
  127.5 119.2 %all-reduce.3.cloned.1.call-done = (bf16[4,256,1024]{2,1,0:T(8,128)(2,1)}, bf16[4,256,1024]{2,1,0:T(8,128)(2,1)}, bf16[4,256,1024]{2,1,0:T(8,128)(2,1)}) async-done(((bf16[4,256,1024]{2,1,0:T(8,128)(2,1)}, bf16[4,256,1024]{2,1,0:T(8,128)(2,1)}, bf16[4,256,1024]{2,1,0:T(8,128)(2,1)}), (bf16[4,256,1024]{2,1,0:T(8,128)(2,1)}, bf16[4,256,1024]{2,1,0:T(8,128)(2,1)}, ...) | async-done | bytes 6291472 | tf_op jit(solution)/shard_map/psum | solution.py:30
  246.7 6.8 %convolution_convert_fusion.6 = bf16[4,256,896]{2,1,0:T(8,128)(2,1)S(1)} fusion(bf16[4,1024,896]{2,1,0:T(8,128)(2,1)} %param.12, bf16[4,256,1024]{2,1,0:T(8,128)(2,1)} %get-tuple-element.5, bf16[4,256,1024]{2,1,0:T(8,128)(2,1)} %get-tuple-element.6), kind=kOutput, calls=%fused_computation.27 | convolution fusion | flops 1888354304 | bytes 13369344 | tf_op jit(solution)/shard_map/erf,efd->erd/dot_general | solution.py:34
  253.6 2.6 copy.104
  256.2 5.5 %all-to-all-start.1 = ((bf16[4,256,896]{2,0,1:T(4,128)(2,1)}), bf16[4,256,896]{2,0,1:T(4,128)(2,1)}, u32[]{:S(2)}, u32[]{:S(2)}) async-start(bf16[4,256,896]{2,0,1:T(4,128)(2,1)} %copy.104), calls=%async_computation.1 | async-start | bytes 3670016 | tf_op jit(solution)/shard_map/all_to_all | solution.py:74
  261.7 4.8 %fusion.3 = bf16[4,256,1024]{2,1,0:T(8,128)(2,1)S(1)} fusion(bf16[4,256,1024]{2,1,0:T(8,128)(2,1)} %get-tuple-element.5, bf16[4,256,1024]{2,1,0:T(8,128)(2,1)} %get-tuple-element.7, bf16[4,256,1024]{2,1,0:T(8,128)(2,1)} %get-tuple-element.6), kind=kLoop, calls=%fused_computation.12 | loop fusion | flops 13631488 | bytes 8388608 | tf_op jit(solution)/shard_map/convert_element_type | solution.py:40
  266.6 5.6 %fusion.19 = f32[4,256,896]{2,1,0:T(8,128)S(1)} fusion(bf16[4,256,1024]{2,1,0:T(8,128)(2,1)S(1)} %fusion.3, bf16[4,896,1024]{2,1,0:T(8,128)(2,1)} %param.10), kind=kOutput, calls=%fused_computation.44 | convolution fusion | flops 1879048192 | bytes 13107200 | tf_op jit(solution)/shard_map/erf,edf->erd/dot_general | solution.py:44
  272.2 5.8 %add_convert_fusion = bf16[4,256,896]{2,1,0:T(8,128)(2,1)S(1)} fusion(f32[4,256,896]{2,1,0:T(8,128)S(1)} %fusion.19, bf16[4,896,1024]{2,1,0:T(8,128)(2,1)} %param.11, bf16[4,256,1024]{2,1,0:T(8,128)(2,1)S(1)} %copy-done.5, bf16[4,256,1024]{2,1,0:T(8,128)(2,1)S(1)} %copy-done.7), kind=kOutput, calls=%fused_computation.19 | convolution fusion | flops 1889271808 | bytes 17039360 | tf_op jit(solution)/shard_map/erf,edf->erd/dot_general | solution.py:45
  278.0 2.6 copy.108
  280.7 23.6 %all-to-all-done.1 = bf16[4,256,896]{2,0,1:T(4,128)(2,1)} async-done(((bf16[4,256,896]{2,0,1:T(4,128)(2,1)}), bf16[4,256,896]{2,0,1:T(4,128)(2,1)}, u32[]{:S(2)}, u32[]{:S(2)}) %all-to-all-start.1) | async-done | bytes 1835040 | tf_op jit(solution)/shard_map/all_to_all | solution.py:74
  304.2 4.6 %all-to-all-start.3 = ((bf16[4,256,896]{2,0,1:T(4,128)(2,1)}), bf16[4,256,896]{2,0,1:T(4,128)(2,1)}, u32[]{:S(2)}, u32[]{:S(2)}) async-start(bf16[4,256,896]{2,0,1:T(4,128)(2,1)} %copy.108), calls=%async_computation.3 | async-start | bytes 3670016 | tf_op jit(solution)/shard_map/all_to_all | solution.py:75
  308.9 6.8 %convolution_convert_fusion.2 = bf16[4,896,1024]{2,1,0:T(8,128)(2,1)} fusion(bf16[4,256,896]{2,1,0:T(8,128)(2,1)} %bitcast.62, bf16[4,256,1024]{2,1,0:T(8,128)(2,1)S(1)} %fusion.3), kind=kOutput, calls=%fused_computation.6 | convolution fusion | flops 1882718208 | bytes 11272192 | tf_op jit(solution)/shard_map/erd,erf->edf/dot_general | solution.py:47
  315.7 5.3 %convolution_convert_fusion.1 = bf16[4,896,1024]{2,1,0:T(8,128)(2,1)} fusion(bf16[4,256,896]{2,1,0:T(8,128)(2,1)S(1)} %bitcast.65, bf16[4,256,1024]{2,1,0:T(8,128)(2,1)S(1)} %copy-done.6, bf16[4,256,1024]{2,1,0:T(8,128)(2,1)S(1)} %copy-done.8), kind=kOutput, calls=%fused_computation.5 | convolution fusion | flops 1891106816 | bytes 13369344 | tf_op jit(solution)/shard_map/erd,erf->edf/dot_general | solution.py:50
  321.1 5.9 %convolution_convert_fusion = bf16[4,1024,896]{2,1,0:T(8,128)(2,1)} fusion(bf16[4,256,896]{2,1,0:T(8,128)(2,1)S(1)} %bitcast.67, bf16[4,256,1024]{2,1,0:T(8,128)(2,1)S(1)} %copy-done.4, bf16[4,256,1024]{2,1,0:T(8,128)(2,1)S(1)} %copy-done.6), kind=kOutput, calls=%fused_computation.4 | convolution fusion | flops 1891106816 | bytes 13369344 | tf_op jit(solution)/shard_map/erf,erd->efd/dot_general | solution.py:53
  326.9 1.7 copy.105
  328.9 1.7 convolution_convert_fusion.10
  330.5 20.4 %all-to-all-done.3 = bf16[4,256,896]{2,0,1:T(4,128)(2,1)} async-done(((bf16[4,256,896]{2,0,1:T(4,128)(2,1)}), bf16[4,256,896]{2,0,1:T(4,128)(2,1)}, u32[]{:S(2)}, u32[]{:S(2)}) %all-to-all-start.3) | async-done | bytes 1835040 | tf_op jit(solution)/shard_map/all_to_all | solution.py:75
  350.9 1.7 copy.109
  352.9 1.7 convolution_convert_fusion.9
  (55 shorter events, 3.9 us)
Async XLA Ops:
  7.2 5.1 %copy-start = (bf16[64,896]{1,0:T(8,128)(2,1)S(1)}, bf16[64,896]{1,0:T(8,128)(2,1)}, u32[]{:S(2)}) copy-start(bf16[64,896]{1,0:T(8,128)(2,1)} %param.7) | copy-start | bytes 344068
  14.2 7.4 %copy-start.12 = (f32[64,8]{0,1:T(8,128)S(1)}, f32[64,8]{0,1:T(8,128)}, u32[]{:S(2)}) copy-start(f32[64,8]{0,1:T(8,128)} %param.9) | copy-start | bytes 6148
  14.2 8.4 %copy-start.11 = (bf16[64,896]{1,0:T(8,128)(2,1)S(1)}, bf16[64,896]{1,0:T(8,128)(2,1)}, u32[]{:S(2)}) copy-start(bf16[64,896]{1,0:T(8,128)(2,1)} %param.13) | copy-start | bytes 344068
  14.2 50.0 %all-to-all-start = ((bf16[32,32,896]{2,1,0:T(8,128)(2,1)}), bf16[32,32,896]{2,1,0:T(8,128)(2,1)S(1)}, u32[]{:S(2)}, u32[]{:S(2)}) async-start(bf16[32,32,896]{2,1,0:T(8,128)(2,1)} %bitcast.59), calls=%async_computation | async-start | bytes 3670016 | tf_op jit(solution)/shard_map/all_to_all | solution.py:67
  64.2 46.6 %all-to-all-start.2 = ((bf16[32,32,896]{2,1,0:T(8,128)(2,1)}), bf16[32,32,896]{2,1,0:T(8,128)(2,1)}, u32[]{:S(2)}, u32[]{:S(2)}) async-start(bf16[32,32,896]{2,1,0:T(8,128)(2,1)} %bitcast.58), calls=%async_computation.2 | async-start | bytes 3670016 | tf_op jit(solution)/shard_map/all_to_all | solution.py:68
  68.5 178.2 %all-reduce.3.cloned.1.call-start = ((), (), s32[]{:S(2)}) async-start(), calls=%async_computation.4 | async-start | bytes 12582912 | tf_op jit(solution)/shard_map/psum | solution.py:30
  70.3 42.3 %copy-start.2 = (bf16[8,4,32,896]{3,2,0,1:T(8,128)(2,1)S(1)}, bf16[8,4,32,896]{3,2,0,1:T(8,128)(2,1)}, u32[]{:S(2)}) copy-start(bf16[8,4,32,896]{3,2,0,1:T(8,128)(2,1)} %copy.103) | copy-start | bytes 5505028
  110.7 9.3 %slice-start = ((s8[7340032]{0:T(1024)(128)(4,1)}), s8[4194304]{0:T(1024)(128)(4,1)S(1)}, s32[]{:S(2)}) async-start(s8[7340032]{0:T(1024)(128)(4,1)} %bitcast.53), calls=%async_computation.5 | async-start | bytes 8388608
  112.6 11.2 %copy-start.9 = (bf16[8,4,32,896]{3,2,0,1:T(8,128)(2,1)}, bf16[8,4,32,896]{3,2,0,1:T(8,128)(2,1)S(1)}, u32[]{:S(2)}) copy-start(bf16[8,4,32,896]{3,2,0,1:T(8,128)(2,1)S(1)} %copy.107) | copy-start | bytes 5505028
  112.6 7.5 %slice-start.1 = ((s8[7340032]{0:T(1024)(128)(4,1)}), s8[3145728]{0:T(1024)(128)(4,1)S(1)}, s32[]{:S(2)}) async-start(s8[7340032]{0:T(1024)(128)(4,1)} %bitcast.53), calls=%async_computation.6 | async-start | bytes 6291456
  112.6 11.2 %slice-start.2 = ((s8[7340032]{0:T(1024)(128)(4,1)}), s8[4194304]{0:T(1024)(128)(4,1)S(1)}, s32[]{:S(2)}) async-start(s8[7340032]{0:T(1024)(128)(4,1)} %bitcast.68), calls=%async_computation.7 | async-start | bytes 8388608
  120.0 3.8 %slice-start.3 = ((s8[7340032]{0:T(1024)(128)(4,1)}), s8[3145728]{0:T(1024)(128)(4,1)S(1)}, s32[]{:S(2)}) async-start(s8[7340032]{0:T(1024)(128)(4,1)} %bitcast.68), calls=%async_computation.8 | async-start | bytes 6291456
  256.2 48.0 %all-to-all-start.1 = ((bf16[4,256,896]{2,0,1:T(4,128)(2,1)}), bf16[4,256,896]{2,0,1:T(4,128)(2,1)}, u32[]{:S(2)}, u32[]{:S(2)}) async-start(bf16[4,256,896]{2,0,1:T(4,128)(2,1)} %copy.104), calls=%async_computation.1 | async-start | bytes 3670016 | tf_op jit(solution)/shard_map/all_to_all | solution.py:74
  266.5 5.6 %copy-start.5 = (bf16[4,256,1024]{2,1,0:T(8,128)(2,1)S(1)}, bf16[4,256,1024]{2,1,0:T(8,128)(2,1)}, u32[]{:S(2)}) copy-start(bf16[4,256,1024]{2,1,0:T(8,128)(2,1)} %get-tuple-element.6) | copy-start | bytes 6291460
  266.5 5.6 %copy-start.7 = (bf16[4,256,1024]{2,1,0:T(8,128)(2,1)S(1)}, bf16[4,256,1024]{2,1,0:T(8,128)(2,1)}, u32[]{:S(2)}) copy-start(bf16[4,256,1024]{2,1,0:T(8,128)(2,1)} %get-tuple-element.7) | copy-start | bytes 6291460
  304.2 46.7 %all-to-all-start.3 = ((bf16[4,256,896]{2,0,1:T(4,128)(2,1)}), bf16[4,256,896]{2,0,1:T(4,128)(2,1)}, u32[]{:S(2)}, u32[]{:S(2)}) async-start(bf16[4,256,896]{2,0,1:T(4,128)(2,1)} %copy.108), calls=%async_computation.3 | async-start | bytes 3670016 | tf_op jit(solution)/shard_map/all_to_all | solution.py:75
  308.8 6.8 %copy-start.3 = (bf16[8,4,32,896]{3,2,0,1:T(8,128)(2,1)S(1)}, bf16[8,4,32,896]{3,2,0,1:T(8,128)(2,1)}, u32[]{:S(2)}) copy-start(bf16[8,4,32,896]{3,2,0,1:T(8,128)(2,1)} %copy.103) | copy-start | bytes 5505028
  308.8 6.8 %copy-start.6 = (bf16[4,256,1024]{2,1,0:T(8,128)(2,1)S(1)}, bf16[4,256,1024]{2,1,0:T(8,128)(2,1)}, u32[]{:S(2)}) copy-start(bf16[4,256,1024]{2,1,0:T(8,128)(2,1)} %get-tuple-element.6) | copy-start | bytes 6291460
  308.8 6.8 %copy-start.8 = (bf16[4,256,1024]{2,1,0:T(8,128)(2,1)S(1)}, bf16[4,256,1024]{2,1,0:T(8,128)(2,1)}, u32[]{:S(2)}) copy-start(bf16[4,256,1024]{2,1,0:T(8,128)(2,1)} %get-tuple-element.7) | copy-start | bytes 6291460
  315.7 5.4 %copy-start.4 = (bf16[4,256,1024]{2,1,0:T(8,128)(2,1)S(1)}, bf16[4,256,1024]{2,1,0:T(8,128)(2,1)}, u32[]{:S(2)}) copy-start(bf16[4,256,1024]{2,1,0:T(8,128)(2,1)} %get-tuple-element.5) | copy-start | bytes 6291460
  315.7 5.4 %copy-start.10 = (bf16[8,4,32,896]{3,2,0,1:T(8,128)(2,1)S(1)}, bf16[8,4,32,896]{3,2,0,1:T(8,128)(2,1)}, u32[]{:S(2)}) copy-start(bf16[8,4,32,896]{3,2,0,1:T(8,128)(2,1)} %copy-done.9) | copy-start | bytes 5505028
  352.6 1.9 copy-start.1
Sparse Core Ops, SparseCore 0:
  127.7 119.0 all-reduce.2
where the time goes:
time: 362 us; the launch traced here: 361 us
  waiting for transfers between devices  242 us (67%)
  matrix products  59.3 us (16%)
  starting transfers between devices  22 us (6%)
  between operations  14.3 us (4%)
  local copies, waits for them, and re-layouts  14.1 us (4%)
  other arithmetic  9.24 us (3%)
    psum x1, waiting for transfers between devices, expert_pass(): lax.psum(up_part.astype(jnp.bfloat16), 'dp').astype(jnp.float32)  119 us
    all_to_all x1, waiting for transfers between devices, body(): lax.all_to_all(send_dy, 'expert', split_axis=0, concat_axis=1, tiled=True)  40.5 us
    all_to_all x1, waiting for transfers between devices, body(): lax.all_to_all(send_in, 'expert', split_axis=0, concat_axis=1, tiled=True)  38.7 us
    all_to_all x1, waiting for transfers between devices, body(): lax.all_to_all(out_rows, 'expert', split_axis=1, concat_axis=0, tiled=True)  23.6 us
    all_to_all x1, waiting for transfers between devices, body(): lax.all_to_all(row_grad, 'expert', split_axis=1, concat_axis=0, tiled=True)  20.4 us
    dot_general x1, matrix products, expert_pass(): jnp.einsum('erd,edf->erf', rows_in, w_up, preferred_element_type=jnp.floa...  7.42 us
    all_to_all x1, starting transfers between devices, body(): lax.all_to_all(send_in, 'expert', split_axis=0, concat_axis=1, tiled=True)  7.38 us
  transfers between devices with their start and end apart: 5, of which 5 were waited for; matrix products, arithmetic and copies ran while one was open for 13% of the time, Pallas kernels for 0%

commit v1 on v0

v1 whole, which is shorter than its diff:
```python
import jax
import jax.numpy as jnp
from jax import lax
from jax.sharding import PartitionSpec as P

EXPERTS = 32
CAP = 32
F32 = jnp.float32
BF16 = jnp.bfloat16


def mm(a, b, dims=((1,), (0,))):
    return lax.dot_general(a, b, (dims, ((), ())), preferred_element_type=F32)


def tables(ids_all, gates_all, first_expert, local_count, blocks):
    tok = ids_all.shape[0] // blocks
    mine = first_expert + jnp.arange(local_count, dtype=jnp.int32)
    hits = ids_all[None, :, :] == mine[:, None, None]
    named = jnp.any(hits, axis=2).reshape(local_count, blocks, tok)
    gate = jnp.sum(jnp.where(hits, gates_all[None], 0.0), axis=2).reshape(local_count, blocks, tok)
    earlier = jnp.triu(jnp.ones((tok, tok), BF16), 1)
    rank = jnp.einsum("ebs,st->ebt", named.astype(BF16), earlier, preferred_element_type=F32)
    slot = jnp.arange(CAP, dtype=jnp.int32)
    block = jnp.arange(blocks, dtype=jnp.int32)
    where = jnp.where(named, rank.astype(jnp.int32), -1)
    pick = (where[:, None, None, :, :] == slot[None, None, :, None, None]) & (
        block[None, :, None, None, None] == block[None, None, None, :, None]
    )
    shape = (local_count * blocks * CAP, blocks * tok)
    weighted = jnp.where(pick, gate[:, None, None, :, :], 0.0)
    row_gate = jnp.sum(weighted, axis=(3, 4)).reshape(-1, 1)
    return pick.astype(BF16).reshape(shape), weighted.astype(BF16).reshape(shape), row_gate


def send(x, axis, pairs):
    return lax.ppermute(x, axis, pairs)


def flip(size, bit):
    return [(i, i ^ bit) for i in range(size)]


def at(x, i):
    return lax.dynamic_index_in_dim(x, i, 0, keepdims=False)


def dp_sum_pair(part, core, n_dp):
    got = send(at(part, 1 - core), "dp", flip(n_dp, 1))
    both = (at(part, core).astype(F32) + got.astype(F32)).astype(BF16)
    far = send(both, "dp", flip(n_dp, 2))
    return both.astype(F32) + far.astype(F32)


def share_pair(x, core, n_dp):
    got = send(x, "dp", flip(n_dp, 1))
    return jnp.where(core == 0, jnp.stack([x, got]), jnp.stack([got, x]))


def return_sum(full, n_ex):
    tok = full.shape[0] // n_ex
    n_z = n_ex // 2
    me = lax.axis_index("expert")
    z, x = me // 2, me % 2
    parts = full.reshape(n_z, 2, tok, full.shape[1])
    got = send(lax.dynamic_index_in_dim(parts, 1 - x, 1, keepdims=False), "expert", flip(n_ex, 1))
    keep = lax.dynamic_index_in_dim(parts, x, 1, keepdims=False)
    col = (keep.astype(F32) + got.astype(F32)).astype(BF16)
    total = at(col, z).astype(F32)
    for k in range(1, n_z):
        to = [(i, (i + 2 * k) % n_ex) for i in range(n_ex)]
        total += send(at(col, (z + k) % n_z), "expert", to).astype(F32)
    return total.astype(BF16)


def make_body(n_dp, n_ex):
    fast = n_dp == 4 and n_ex == 8

    def body(tokens, expert_ids, gate_weights, w_gate, w_up, w_down, cotangent):
        width = tokens.shape[1]
        count = w_gate.shape[0]
        rows = n_ex * CAP
        core = lax.axis_index("dp") % 2
        route = jnp.concatenate([expert_ids.astype(F32), gate_weights], axis=1)
        route = lax.all_gather(route, "expert", axis=0, tiled=True)
        top = expert_ids.shape[1]
        both = jnp.concatenate([tokens, cotangent], axis=1)
        both = lax.all_gather(both, "expert", axis=0, tiled=True)
        pick, weighted, row_gate = tables(
            route[:, :top].astype(jnp.int32),
            route[:, top:],
            lax.axis_index("expert") * count,
            count,
            n_ex,
        )
        picked = mm(pick, both)
        rows_in = picked[:, :width].astype(BF16).reshape(count, rows, width)
        rows_dy = (picked[:, width:] * row_gate).astype(BF16).reshape(count, rows, width)

        def gate_up(e, w):
            return mm(rows_in[e], w[e]).astype(BF16)

        def back(e):
            return mm(rows_dy[e], w_down[e], ((1,), (1,))).astype(BF16)

        def forward(gate_sum, up_sum):
            logistic = jax.nn.sigmoid(gate_sum)
            return (gate_sum * logistic * up_sum).astype(BF16)

        def backward(gate_sum, up_sum, hidden_grad):
            logistic = jax.nn.sigmoid(gate_sum)
            up_grad = (hidden_grad * gate_sum * logistic).astype(BF16)
            gate_grad = (
                hidden_grad * up_sum * logistic * (1.0 + gate_sum * (1.0 - logistic))
            ).astype(BF16)
            return gate_grad, up_grad

        if fast:
            halves = range(0, count, 2)
            sums = []
            for e in halves:
                g = dp_sum_pair(jnp.stack([gate_up(e, w_gate), gate_up(e + 1, w_gate)]), core, n_dp)
                u = dp_sum_pair(jnp.stack([gate_up(e, w_up), gate_up(e + 1, w_up)]), core, n_dp)
                sums.append((g, u))
            grads = [dp_sum_pair(jnp.stack([back(e), back(e + 1)]), core, n_dp) for e in halves]
            hidden = jnp.concatenate([share_pair(forward(g, u), core, n_dp) for g, u in sums])
            pairs = [
                share_pair(jnp.stack(backward(g, u, h)), core, n_dp)
                for (g, u), h in zip(sums, grads)
            ]
            gate_grad = jnp.concatenate([p[:, 0] for p in pairs])
            up_grad = jnp.concatenate([p[:, 1] for p in pairs])
        else:
            gate_sum, up_sum, hidden_grad = (
                lax.psum(jnp.stack(p), "dp").astype(F32)
                for p in (
                    [gate_up(e, w_gate) for e in range(count)],
                    [gate_up(e, w_up) for e in range(count)],
                    [back(e) for e in range(count)],
                )
            )
            hidden = forward(gate_sum, up_sum)
            gate_grad, up_grad = backward(gate_sum, up_sum, hidden_grad)

        out_rows = jnp.concatenate([mm(hidden[e], w_down[e]).astype(BF16) for e in range(count)])
        mixed = mm(weighted, out_rows, ((0,), (0,))).astype(BF16)
        row_grad = jnp.concatenate(
            [
                (
                    mm(gate_grad[e], w_gate[e], ((1,), (1,))) + mm(up_grad[e], w_up[e], ((1,), (1,)))
                ).astype(BF16)
                for e in range(count)
            ]
        )
        token_grad = mm(pick, row_grad, ((0,), (0,))).astype(BF16)
        if fast:
            mixed, token_grad = return_sum(mixed, n_ex), return_sum(token_grad, n_ex)
        else:
            mixed, token_grad = (
                lax.psum_scatter(v, "expert", scatter_dimension=0, tiled=True)
                for v in (mixed, token_grad)
            )
        grad_gate = jnp.einsum(
            "erd,erf->edf", rows_in, gate_grad, preferred_element_type=F32
        ).astype(BF16)
        grad_up = jnp.einsum(
            "erd,erf->edf", rows_in, up_grad, preferred_element_type=F32
        ).astype(BF16)
        grad_down = jnp.einsum(
            "erf,erd->efd", hidden, rows_dy, preferred_element_type=F32
        ).astype(BF16)
        return mixed, token_grad, grad_gate, grad_up, grad_down

    return body


def solution(mesh):
    placed = (
        P("expert", "dp"),
        P("expert", None),
        P("expert", None),
        P("expert", "dp", None),
        P("expert", "dp", None),
        P("expert", None, "dp"),
        P("expert", "dp"),
    )
    return jax.shard_map(
        make_body(mesh.shape["dp"], mesh.shape["expert"]),
        mesh=mesh,
        in_specs=placed,
        out_specs=(
            P("expert", "dp"),
            P("expert", "dp"),
            P("expert", "dp", None),
            P("expert", "dp", None),
            P("expert", None, "dp"),
        ),
        check_vma=False,
    )
```

time: 362 us -> 225 us (0.62)
  waiting for transfers between devices: 242 us -> 70.9 us
  blocking collectives: 0 us -> 32.5 us
  other arithmetic: 9.24 us -> 22.2 us
  matrix products: 59.3 us -> 47.5 us
    all_to_all x4 -> x0, waiting for transfers between devices: 123 us -> none  [the longest x1 40.5 us: body(): lax.all_to_all(send_dy, 'expert', split_axis=0, concat_axis=1, tiled=True)]
    psum x1 -> x0, waiting for transfers between devices: 119 us -> none  [expert_pass(): lax.psum(up_part.astype(jnp.bfloat16), 'dp').astype(jnp.float32)]
    ppermute x0 -> x24, waiting for transfers between devices: none -> 60.4 us  [send(): return lax.ppermute(x, axis, pairs)]
    all_gather x0 -> x1, blocking collectives: none -> 32.5 us  [body(): route = lax.all_gather(route, 'expert', axis=0, tiled=True)]
    all_to_all x4 -> x0, starting transfers between devices: 21.8 us -> none  [the longest x1 7.38 us: body(): lax.all_to_all(send_in, 'expert', split_axis=0, concat_axis=1, tiled=True)]
    ppermute x0 -> x24, starting transfers between devices: none -> 20.2 us  [send(): return lax.ppermute(x, axis, pairs)]
    dot_general x13 -> x31, matrix products: 59.3 us -> 47.5 us  [the longest x27 31.6 us: mm(): return lax.dot_general(a, b, (dims, ((), ())), preferred_element_type=F32)]
    all_gather x0 -> x1, waiting for transfers between devices: none -> 10.5 us  [body(): both = lax.all_gather(both, 'expert', axis=0, tiled=True)]
  transfers between devices with their start and end apart: 5 -> 25, of which waited for: 5 -> 9; matrix products, arithmetic and copies ran while one was open for 13% -> 27% of each run, Pallas kernels for 0% -> 0%
where the time goes in v1:
time: 225 us; the launch traced here: 221 us
  waiting for transfers between devices  70.9 us (32%)
  matrix products  47.5 us (21%)
  blocking collectives  32.5 us (14%)
  other arithmetic  22.2 us (10%)
  starting transfers between devices  20.2 us (9%)
  between operations  15.2 us (7%)
  local copies, waits for them, and re-layouts  13 us (6%)
    ppermute x24, waiting for transfers between devices, send(): return lax.ppermute(x, axis, pairs)  60.4 us
    all_gather x1, blocking collectives, body(): route = lax.all_gather(route, 'expert', axis=0, tiled=True)  32.5 us
    dot_general x27, matrix products, mm(): return lax.dot_general(a, b, (dims, ((), ())), preferred_element_type=F32)  31.6 us
    ppermute x24, starting transfers between devices, send(): return lax.ppermute(x, axis, pairs)  20.2 us
    all_gather x1, waiting for transfers between devices, body(): both = lax.all_gather(both, 'expert', axis=0, tiled=True)  10.5 us
    broadcast_in_dim x3, local copies, waits for them, and re-layouts, tables(): weighted = jnp.where(pick, gate[:, None, None, :, :], 0.0)  5.84 us
    convert_element_type x6, other arithmetic, dp_sum_pair(): both = (at(part, core).astype(F32) + got.astype(F32)).astype(BF16)  5.52 us
    dot_general x1, matrix products, body(): jnp.einsum('erf,erd->efd', hidden, rows_dy, preferred_element_type=F32)  5.45 us
  transfers between devices with their start and end apart: 25, of which 9 were waited for; matrix products, arithmetic and copies ran while one was open for 27% of the time, Pallas kernels for 0%

profile of v1, /device:TPU:0, one launch (start us, length us, event | category | flops | bytes accessed | tf_op | source)
XLA Modules:
  0.0 221.4 jit_solution(3917922648879700936)
XLA Ops:
  7.2 1.7 pad_maximum_fusion.2
  10.3 32.5 %all-gather = f32[8,64,16]{1,2,0:T(8,128)S(1)} all-gather(f32[1,64,16]{1,2,0:T(8,128)S(1)} %maximum_bitcast_fusion), channel_id=1, replica_groups=mesh['dp'=4,'expert'=8] {'expert'}, dimensions={0}, use_global_device_ids=true | all-gather | bytes 36864 | tf_op jit(solution)/shard_map/all_gather | solution.py:85
  43.4 3.1 %select_reduce_fusion = f32[4,8,32]{2,1,0:T(8,128)S(1)} fusion(f32[4,8,64]{2,1,0:T(8,128)S(1)} %broadcast_in_dim.53, pred[8,8]{1,0:T(8,128)(4,1)S(1)} %iota_compare_fusion.2, pred[4,32,8,64]{3,2,1,0:T(8,128)(4,1)S(1)} %iota_compare_fusion), kind=kLoop, calls=%fused_computation.3 | loop fusion | flops 1571840 | bytes 77888 | tf_op jit(solution)/shard_map/reduce_sum | solution.py:32
  47.3 2.2 and.54
  49.5 10.5 %all-gather.3.cloned.1.call-done = bf16[512,1792]{1,0:T(8,128)(2,1)} async-done(((bf16[64,1792]{1,0:T(8,128)(2,1)}), bf16[512,1792]{1,0:T(8,128)(2,1)}) %all-gather.3.cloned.1.call-update) | async-done | bytes 1835024 | tf_op jit(solution)/shard_map/all_gather | solution.py:88
  60.1 3.6 %fusion.285 = (bf16[1024,1792]{1,0:T(8,128)(2,1)S(1)}, f32[1024,1792]{1,0:T(8,128)S(1)}) fusion(pred[1024,512]{1,0:T(32,128)(4,1)S(1)} %and.54, bf16[512,1792]{1,0:T(8,128)(2,1)} %all-gather.3.cloned.1.call-done), kind=kOutput, calls=%fused_computation.303 | convolution fusion | flops 1880883200 | bytes 13369344 | tf_op jit(solution)/shard_map/dot_general | solution.py:13
  63.9 3.7 %fusion.176 = bf16[1,256,1024]{2,1,0:T(8,128)(2,1)S(1)} fusion(bf16[4,1024,896]{2,1,0:T(8,128)(2,1)} %param.12, bf16[1024,896]{1,0:T(8,128)(2,1)S(1)} %fusion), kind=kOutput, calls=%fused_computation.133 | convolution fusion | flops 470024192 | bytes 2818048 | tf_op jit(solution)/shard_map/dot_general | solution.py:13
  67.7 2.4 %fusion.179 = bf16[1,256,1024]{2,1,0:T(8,128)(2,1)S(1)} fusion(bf16[4,1024,896]{2,1,0:T(8,128)(2,1)} %param.12, bf16[1024,896]{1,0:T(8,128)(2,1)S(1)} %fusion), kind=kOutput, calls=%fused_computation.134 | convolution fusion | flops 470024192 | bytes 2818048 | tf_op jit(solution)/shard_map/dot_general | solution.py:13
  70.1 2.2 %fusion.194 = bf16[1,256,1024]{2,1,0:T(8,128)(2,1)S(1)} fusion(bf16[4,1024,896]{2,1,0:T(8,128)(2,1)} %param.12, bf16[1024,896]{1,0:T(8,128)(2,1)S(1)} %fusion), kind=kOutput, calls=%fused_computation.139 | convolution fusion | flops 470024192 | bytes 2818048 | tf_op jit(solution)/shard_map/dot_general | solution.py:13
  72.3 2.4 %fusion.197 = bf16[1,256,1024]{2,1,0:T(8,128)(2,1)S(1)} fusion(bf16[4,1024,896]{2,1,0:T(8,128)(2,1)} %param.12, bf16[1024,896]{1,0:T(8,128)(2,1)S(1)} %fusion), kind=kOutput, calls=%fused_computation.140 | convolution fusion | flops 470024192 | bytes 2818048 | tf_op jit(solution)/shard_map/dot_general | solution.py:13
  84.0 1.5 collective-permute-start.18
  87.7 1.5 collective-permute-start.8
  92.3 1.5 collective-permute-start.3
  94.9 4.0 %collective-permute-done.18 = bf16[256,1024]{1,0:T(8,128)(2,1)S(1)} collective-permute-done((bf16[256,1024]{1,0:T(8,128)(2,1)S(1)}, bf16[256,1024]{1,0:T(8,128)(2,1)S(1)}, u32[]{:S(2)}, u32[]{:S(2)}) %collective-permute-start.18) | collective-permute-done | bytes 524320 | tf_op jit(solution)/shard_map/ppermute | solution.py:37
  101.2 1.7 broadcast_in_dim.54
  102.9 4.0 %broadcast_in_dim.55 = bf16[1024,512]{1,0:T(8,128)(2,1)} reshape(bf16[4,8,32,8,64]{4,3,2,1,0:T(8,128)(2,1)} %broadcast_in_dim.54) | data formatting | bytes 2097152 | tf_op jit(solution)/shard_map/jit(_where)/broadcast_in_dim | solution.py:31
  106.9 1.7 slice.228
  108.7 12.8 %collective-permute-done.8 = bf16[256,1024]{1,0:T(8,128)(2,1)} collective-permute-done((bf16[256,1024]{1,0:T(8,128)(2,1)}, bf16[256,1024]{1,0:T(8,128)(2,1)}, u32[]{:S(2)}, u32[]{:S(2)}) %collective-permute-start.8) | collective-permute-done | bytes 524320 | tf_op jit(solution)/shard_map/ppermute | solution.py:37
  121.5 11.2 %collective-permute-done.6 = bf16[256,1024]{1,0:T(8,128)(2,1)} collective-permute-done((bf16[256,1024]{1,0:T(8,128)(2,1)}, bf16[256,1024]{1,0:T(8,128)(2,1)}, u32[]{:S(2)}, u32[]{:S(2)}) %collective-permute-start.6) | collective-permute-done | bytes 524320 | tf_op jit(solution)/shard_map/ppermute | solution.py:37
  132.7 2.5 %fusion.249 = (bf16[1,256,1024]{2,1,0:T(8,128)(2,1)S(1)}, bf16[256,1024]{1,0:T(8,128)(2,1)S(1)}, bf16[1,256,1024]{2,1,0:T(8,128)(2,1)S(1)}) fusion(bf16[256,1024]{1,0:T(8,128)(2,1)} %collective-permute-done.6, bf16[256,1024]{1,0:T(8,128)(2,1)} %fusion.216, bf16[256,1024]{1,0:T(8,128)(2,1)} %collective-permute-done.8, bf16[256,1024]{1,0:T(8,128)(2,1)} %fusion.215, ...), kind=kLoop, calls=%fused_computation.250 | loop fusion | flops 6553600 | bytes 4718592 | tf_op jit(solution)/shard_map/stack | solution.py:128
  135.3 8.6 %collective-permute-done.3 = bf16[256,1024]{1,0:T(8,128)(2,1)} collective-permute-done((bf16[256,1024]{1,0:T(8,128)(2,1)}, bf16[256,1024]{1,0:T(8,128)(2,1)}, u32[]{:S(2)}, u32[]{:S(2)}) %collective-permute-start.3) | collective-permute-done | bytes 524320 | tf_op jit(solution)/shard_map/ppermute | solution.py:37
  143.9 10.3 %collective-permute-done.1 = bf16[256,1024]{1,0:T(8,128)(2,1)} collective-permute-done((bf16[256,1024]{1,0:T(8,128)(2,1)}, bf16[256,1024]{1,0:T(8,128)(2,1)}, u32[]{:S(2)}, u32[]{:S(2)}) %collective-permute-start.1) | collective-permute-done | bytes 524320 | tf_op jit(solution)/shard_map/ppermute | solution.py:37
  154.2 2.5 %fusion.248 = (bf16[1,256,1024]{2,1,0:T(8,128)(2,1)S(1)}, bf16[256,1024]{1,0:T(8,128)(2,1)S(1)}, bf16[1,256,1024]{2,1,0:T(8,128)(2,1)S(1)}) fusion(bf16[256,1024]{1,0:T(8,128)(2,1)} %collective-permute-done.1, bf16[256,1024]{1,0:T(8,128)(2,1)} %fusion.218, bf16[256,1024]{1,0:T(8,128)(2,1)} %collective-permute-done.3, bf16[256,1024]{1,0:T(8,128)(2,1)} %fusion.217, ...), kind=kLoop, calls=%fused_computation.249 | loop fusion | flops 6553600 | bytes 4718592 | tf_op jit(solution)/shard_map/stack | solution.py:128
  163.6 5.4 %convolution_convert_fusion = bf16[4,1024,896]{2,1,0:T(8,128)(2,1)} fusion(bf16[4,256,896]{2,1,0:T(8,128)(2,1)S(1)} %bitcast.318, bf16[2,256,1024]{2,1,0:T(8,128)(2,1)S(1)} %maximum_select_fusion.3, bf16[2,256,1024]{2,1,0:T(8,128)(2,1)S(1)} %maximum_select_fusion.2), kind=kOutput, calls=%fused_computation | convolution fusion | flops 1883766784 | bytes 11272192 | tf_op jit(solution)/shard_map/erf,erd->efd/dot_general | solution.py:169
  169.0 6.2 %collective-permute-done.10 = bf16[4,64,896]{2,1,0:T(8,128)(2,1)S(1)} collective-permute-done((bf16[4,64,896]{2,1,0:T(8,128)(2,1)S(1)}, bf16[4,64,896]{2,1,0:T(8,128)(2,1)S(1)}, u32[]{:S(2)}, u32[]{:S(2)}) %collective-permute-start.10) | collective-permute-done | bytes 458784 | tf_op jit(solution)/shard_map/ppermute | solution.py:37
  175.4 2.1 collective-permute-start.11
  177.5 2.0 collective-permute-start.13
  190.6 5.2 %convolution_convert_fusion.1 = bf16[4,896,1024]{2,1,0:T(8,128)(2,1)} fusion(bf16[4,256,896]{2,1,0:T(8,128)(2,1)S(1)} %bitcast.316, bf16[2,256,1024]{2,1,0:T(8,128)(2,1)S(1)} %get-tuple-element.7, bf16[2,256,1024]{2,1,0:T(8,128)(2,1)S(1)} %get-tuple-element.5), kind=kOutput, calls=%fused_computation.1 | convolution fusion | flops 1883766784 | bytes 11272192 | tf_op jit(solution)/shard_map/erd,erf->edf/dot_general | solution.py:166
  195.7 5.2 %convolution_convert_fusion.2 = bf16[4,896,1024]{2,1,0:T(8,128)(2,1)} fusion(bf16[4,256,896]{2,1,0:T(8,128)(2,1)S(1)} %bitcast.317, bf16[2,256,1024]{2,1,0:T(8,128)(2,1)S(1)} %get-tuple-element.8, bf16[2,256,1024]{2,1,0:T(8,128)(2,1)S(1)} %get-tuple-element.6), kind=kOutput, calls=%fused_computation.2 | convolution fusion | flops 1883766784 | bytes 11272192 | tf_op jit(solution)/shard_map/erd,erf->edf/dot_general | solution.py:163
  201.7 3.3 %collective-permute-start.23 = (bf16[64,896]{1,0:T(8,128)(2,1)S(1)}, bf16[64,896]{1,0:T(8,128)(2,1)S(1)}, u32[]{:S(2)}, u32[]{:S(2)}) collective-permute-start(bf16[64,896]{1,0:T(8,128)(2,1)S(1)} %get-tuple-element.20), channel_id=1, source_target_pairs={{0,6},{1,7},{2,0},{3,1},{4,2},{5,3},{6,4},{7,5},{8,14},{9,15},{10,... | collective-permute-start | bytes 344072 | tf_op jit(solution)/shard_map/ppermute | solution.py:37
  206.2 2.4 %collective-permute-done.21 = bf16[64,896]{1,0:T(8,128)(2,1)S(1)} collective-permute-done((bf16[64,896]{1,0:T(8,128)(2,1)S(1)}, bf16[64,896]{1,0:T(8,128)(2,1)S(1)}, u32[]{:S(2)}, u32[]{:S(2)}) %collective-permute-start.21) | collective-permute-done | bytes 114720 | tf_op jit(solution)/shard_map/ppermute | solution.py:37
  208.6 4.8 %collective-permute-done.22 = bf16[64,896]{1,0:T(8,128)(2,1)S(1)} collective-permute-done((bf16[64,896]{1,0:T(8,128)(2,1)S(1)}, bf16[64,896]{1,0:T(8,128)(2,1)S(1)}, u32[]{:S(2)}, u32[]{:S(2)}) %collective-permute-start.22) | collective-permute-done | bytes 114720 | tf_op jit(solution)/shard_map/ppermute | solution.py:37
  (135 shorter events, 41.4 us)
Async XLA Ops:
  7.2 52.9 %all-gather.3.cloned.1.call-start = ((), (), s32[]{:S(2)}) async-start(), calls=%async_computation | async-start | bytes 2064384 | tf_op jit(solution)/shard_map/all_gather | solution.py:88
  63.6 18.6 %copy-start = (bf16[1024,1792]{1,0:T(8,128)(2,1)}, bf16[1024,1792]{1,0:T(8,128)(2,1)S(1)}, u32[]{:S(2)}) copy-start(bf16[1024,1792]{1,0:T(8,128)(2,1)S(1)} %get-tuple-element.27) | copy-start | bytes 11010052
  63.6 11.1 %slice-start.2 = ((s8[7340032]{0:T(1024)(128)(4,1)}), s8[3145728]{0:T(1024)(128)(4,1)S(1)}, s32[]{:S(2)}) async-start(s8[7340032]{0:T(1024)(128)(4,1)} %bitcast.331), calls=%async_computation.3 | async-start | bytes 6291456
  79.3 3.8 %collective-permute-start.17 = (bf16[256,1024]{1,0:T(8,128)(2,1)S(1)}, bf16[256,1024]{1,0:T(8,128)(2,1)S(1)}, u32[]{:S(2)}, u32[]{:S(2)}) collective-permute-start(bf16[256,1024]{1,0:T(8,128)(2,1)S(1)} %fusion.223), channel_id=1, source_target_pairs={{0,8},{8,0},{16,24},{24,16},{1,9},{9,1},{17,25},{25,17},{2,10},{10... | collective-permute-start | bytes 1572872 | tf_op jit(solution)/shard_map/ppermute | solution.py:37
  79.6 4.4 %collective-permute-start.14 = (bf16[256,1024]{1,0:T(8,128)(2,1)S(1)}, bf16[256,1024]{1,0:T(8,128)(2,1)S(1)}, u32[]{:S(2)}, u32[]{:S(2)}) collective-permute-start(bf16[256,1024]{1,0:T(8,128)(2,1)S(1)} %fusion.227), channel_id=1, source_target_pairs={{0,8},{8,0},{16,24},{24,16},{1,9},{9,1},{17,25},{25,17},{2,10},{10... | collective-permute-start | bytes 1572872 | tf_op jit(solution)/shard_map/ppermute | solution.py:37
  80.3 10.0 %collective-permute-start.2 = (bf16[256,1024]{1,0:T(8,128)(2,1)S(1)}, bf16[256,1024]{1,0:T(8,128)(2,1)S(1)}, u32[]{:S(2)}, u32[]{:S(2)}) collective-permute-start(bf16[256,1024]{1,0:T(8,128)(2,1)S(1)} %fusion.239), channel_id=1, source_target_pairs={{0,8},{8,0},{16,24},{24,16},{1,9},{9,1},{17,25},{25,17},{2,10},{10... | collective-permute-start | bytes 1572872 | tf_op jit(solution)/shard_map/ppermute | solution.py:37
  80.6 5.3 %collective-permute-start.7 = (bf16[256,1024]{1,0:T(8,128)(2,1)S(1)}, bf16[256,1024]{1,0:T(8,128)(2,1)S(1)}, u32[]{:S(2)}, u32[]{:S(2)}) collective-permute-start(bf16[256,1024]{1,0:T(8,128)(2,1)S(1)} %fusion.231), channel_id=1, source_target_pairs={{0,8},{8,0},{16,24},{24,16},{1,9},{9,1},{17,25},{25,17},{2,10},{10... | collective-permute-start | bytes 1572872 | tf_op jit(solution)/shard_map/ppermute | solution.py:37
  81.4 6.3 %collective-permute-start.5 = (bf16[256,1024]{1,0:T(8,128)(2,1)S(1)}, bf16[256,1024]{1,0:T(8,128)(2,1)S(1)}, u32[]{:S(2)}, u32[]{:S(2)}) collective-permute-start(bf16[256,1024]{1,0:T(8,128)(2,1)S(1)} %fusion.235), channel_id=1, source_target_pairs={{0,8},{8,0},{16,24},{24,16},{1,9},{9,1},{17,25},{25,17},{2,10},{10... | collective-permute-start | bytes 1572872 | tf_op jit(solution)/shard_map/ppermute | solution.py:37
  83.1 9.1 %collective-permute-start = (bf16[256,1024]{1,0:T(8,128)(2,1)S(1)}, bf16[256,1024]{1,0:T(8,128)(2,1)S(1)}, u32[]{:S(2)}, u32[]{:S(2)}) collective-permute-start(bf16[256,1024]{1,0:T(8,128)(2,1)S(1)} %fusion.243), channel_id=1, source_target_pairs={{0,8},{8,0},{16,24},{24,16},{1,9},{9,1},{17,25},{25,17},{2,10},{10... | collective-permute-start | bytes 1572872 | tf_op jit(solution)/shard_map/ppermute | solution.py:37
  84.0 14.9 %collective-permute-start.18 = (bf16[256,1024]{1,0:T(8,128)(2,1)S(1)}, bf16[256,1024]{1,0:T(8,128)(2,1)S(1)}, u32[]{:S(2)}, u32[]{:S(2)}) collective-permute-start(bf16[256,1024]{1,0:T(8,128)(2,1)S(1)} %fusion.213), channel_id=1, source_target_pairs={{0,16},{8,24},{16,0},{24,8},{1,17},{9,25},{17,1},{25,9},{2,18},{10... | collective-permute-start | bytes 1572872 | tf_op jit(solution)/shard_map/ppermute | solution.py:37
  85.9 49.4 %collective-permute-start.15 = (bf16[256,1024]{1,0:T(8,128)(2,1)S(1)}, bf16[256,1024]{1,0:T(8,128)(2,1)}, u32[]{:S(2)}, u32[]{:S(2)}) collective-permute-start(bf16[256,1024]{1,0:T(8,128)(2,1)S(1)} %fusion.214), channel_id=1, source_target_pairs={{0,16},{8,24},{16,0},{24,8},{1,17},{9,25},{17,1},{25,9},{2,18},{10... | collective-permute-start | bytes 1572872 | tf_op jit(solution)/shard_map/ppermute | solution.py:37
  87.7 33.8 %collective-permute-start.8 = (bf16[256,1024]{1,0:T(8,128)(2,1)}, bf16[256,1024]{1,0:T(8,128)(2,1)}, u32[]{:S(2)}, u32[]{:S(2)}) collective-permute-start(bf16[256,1024]{1,0:T(8,128)(2,1)} %fusion.215), channel_id=1, source_target_pairs={{0,16},{8,24},{16,0},{24,8},{1,17},{9,25},{17,1},{25,9},{2,18},{10... | collective-permute-start | bytes 1572872 | tf_op jit(solution)/shard_map/ppermute | solution.py:37
  90.3 42.4 %collective-permute-start.6 = (bf16[256,1024]{1,0:T(8,128)(2,1)}, bf16[256,1024]{1,0:T(8,128)(2,1)}, u32[]{:S(2)}, u32[]{:S(2)}) collective-permute-start(bf16[256,1024]{1,0:T(8,128)(2,1)} %fusion.216), channel_id=1, source_target_pairs={{0,16},{8,24},{16,0},{24,8},{1,17},{9,25},{17,1},{25,9},{2,18},{10... | collective-permute-start | bytes 1572872 | tf_op jit(solution)/shard_map/ppermute | solution.py:37
  92.3 51.7 %collective-permute-start.3 = (bf16[256,1024]{1,0:T(8,128)(2,1)}, bf16[256,1024]{1,0:T(8,128)(2,1)}, u32[]{:S(2)}, u32[]{:S(2)}) collective-permute-start(bf16[256,1024]{1,0:T(8,128)(2,1)} %fusion.217), channel_id=1, source_target_pairs={{0,16},{8,24},{16,0},{24,8},{1,17},{9,25},{17,1},{25,9},{2,18},{10... | collective-permute-start | bytes 1572872 | tf_op jit(solution)/shard_map/ppermute | solution.py:37
  99.7 54.5 %collective-permute-start.1 = (bf16[256,1024]{1,0:T(8,128)(2,1)}, bf16[256,1024]{1,0:T(8,128)(2,1)}, u32[]{:S(2)}, u32[]{:S(2)}) collective-permute-start(bf16[256,1024]{1,0:T(8,128)(2,1)} %fusion.218), channel_id=1, source_target_pairs={{0,16},{8,24},{16,0},{24,8},{1,17},{9,25},{17,1},{25,9},{2,18},{10... | collective-permute-start | bytes 1572872 | tf_op jit(solution)/shard_map/ppermute | solution.py:37
  106.9 25.8 %copy-start.3 = (bf16[256,1024]{1,0:T(8,128)(2,1)S(1)}, bf16[256,1024]{1,0:T(8,128)(2,1)}, u32[]{:S(2)}) copy-start(bf16[256,1024]{1,0:T(8,128)(2,1)} %copy-done.2) | copy-start | bytes 1572868
  132.7 25.0 %slice-start = ((s8[7340032]{0:T(1024)(128)(4,1)}), s8[4194304]{0:T(1024)(128)(4,1)S(1)}, s32[]{:S(2)}) async-start(s8[7340032]{0:T(1024)(128)(4,1)} %bitcast.329), calls=%async_computation.1 | async-start | bytes 8388608
  135.2 22.5 %slice-start.1 = ((s8[7340032]{0:T(1024)(128)(4,1)}), s8[3145728]{0:T(1024)(128)(4,1)S(1)}, s32[]{:S(2)}) async-start(s8[7340032]{0:T(1024)(128)(4,1)} %bitcast.329), calls=%async_computation.2 | async-start | bytes 6291456
  135.3 22.3 %collective-permute-start.9 = (bf16[256,1024]{1,0:T(8,128)(2,1)S(1)}, bf16[256,1024]{1,0:T(8,128)(2,1)S(1)}, u32[]{:S(2)}, u32[]{:S(2)}) collective-permute-start(bf16[256,1024]{1,0:T(8,128)(2,1)S(1)} %get-tuple-element.13), channel_id=1, source_target_pairs={{0,8},{8,0},{16,24},{24,16},{1,9},{9,1},{17,25},{25,17},{2,10},{10... | collective-permute-start | bytes 1572872 | tf_op jit(solution)/shard_map/ppermute | solution.py:37
  156.8 2.4 %collective-permute-start.4 = (bf16[256,1024]{1,0:T(8,128)(2,1)S(1)}, bf16[256,1024]{1,0:T(8,128)(2,1)S(1)}, u32[]{:S(2)}, u32[]{:S(2)}) collective-permute-start(bf16[256,1024]{1,0:T(8,128)(2,1)S(1)} %get-tuple-element.10), channel_id=1, source_target_pairs={{0,8},{8,0},{16,24},{24,16},{1,9},{9,1},{17,25},{25,17},{2,10},{10... | collective-permute-start | bytes 1572872 | tf_op jit(solution)/shard_map/ppermute | solution.py:37
  157.0 23.1 %collective-permute-start.19 = (bf16[2,256,1024]{2,1,0:T(8,128)(2,1)S(1)}, bf16[2,256,1024]{2,1,0:T(8,128)(2,1)S(1)}, u32[]{:S(2)}, u32[]{:S(2)}) collective-permute-start(bf16[2,256,1024]{2,1,0:T(8,128)(2,1)S(1)} %get-tuple-element.18), channel_id=1, source_target_pairs={{0,8},{8,0},{16,24},{24,16},{1,9},{9,1},{17,25},{25,17},{2,10},{10... | collective-permute-start | bytes 3145736 | tf_op jit(solution)/shard_map/ppermute | solution.py:37
  162.7 12.5 %collective-permute-start.10 = (bf16[4,64,896]{2,1,0:T(8,128)(2,1)S(1)}, bf16[4,64,896]{2,1,0:T(8,128)(2,1)S(1)}, u32[]{:S(2)}, u32[]{:S(2)}) collective-permute-start(bf16[4,64,896]{2,1,0:T(8,128)(2,1)S(1)} %dynamic-slice_bitcast_fusion.1), channel_id=1, source_target_pairs={{0,1},{1,0},{2,3},{3,2},{4,5},{5,4},{6,7},{7,6},{8,9},{9,8},{10,11... | collective-permute-start | bytes 1376264 | tf_op jit(solution)/shard_map/ppermute | solution.py:37
  163.3 17.3 %slice-start.4 = ((s8[7340032]{0:T(1024)(128)(4,1)}), s8[4194304]{0:T(1024)(128)(4,1)S(1)}, s32[]{:S(2)}) async-start(s8[7340032]{0:T(1024)(128)(4,1)} %bitcast.333), calls=%async_computation.5 | async-start | bytes 8388608
  163.5 18.8 %collective-permute-start.16 = (bf16[2,256,1024]{2,1,0:T(8,128)(2,1)S(1)}, bf16[2,256,1024]{2,1,0:T(8,128)(2,1)S(1)}, u32[]{:S(2)}, u32[]{:S(2)}) collective-permute-start(bf16[2,256,1024]{2,1,0:T(8,128)(2,1)S(1)} %get-tuple-element.16), channel_id=1, source_target_pairs={{0,8},{8,0},{16,24},{24,16},{1,9},{9,1},{17,25},{25,17},{2,10},{10... | collective-permute-start | bytes 3145736 | tf_op jit(solution)/shard_map/ppermute | solution.py:37
  163.6 17.1 %slice-start.5 = ((s8[7340032]{0:T(1024)(128)(4,1)}), s8[3145728]{0:T(1024)(128)(4,1)S(1)}, s32[]{:S(2)}) async-start(s8[7340032]{0:T(1024)(128)(4,1)} %bitcast.333), calls=%async_computation.6 | async-start | bytes 6291456
  175.4 29.6 %collective-permute-start.11 = (bf16[64,896]{1,0:T(8,128)(2,1)S(1)}, bf16[64,896]{1,0:T(8,128)(2,1)S(1)}, u32[]{:S(2)}, u32[]{:S(2)}) collective-permute-start(bf16[64,896]{1,0:T(8,128)(2,1)S(1)} %get-tuple-element.22), channel_id=1, source_target_pairs={{0,2},{1,3},{2,4},{3,5},{4,6},{5,7},{6,0},{7,1},{8,10},{9,11},{10,... | collective-permute-start | bytes 344072 | tf_op jit(solution)/shard_map/ppermute | solution.py:37
  177.5 28.0 %collective-permute-start.13 = (bf16[64,896]{1,0:T(8,128)(2,1)S(1)}, bf16[64,896]{1,0:T(8,128)(2,1)S(1)}, u32[]{:S(2)}, u32[]{:S(2)}) collective-permute-start(bf16[64,896]{1,0:T(8,128)(2,1)S(1)} %get-tuple-element.23), channel_id=1, source_target_pairs={{0,6},{1,7},{2,0},{3,1},{4,2},{5,3},{6,4},{7,5},{8,14},{9,15},{10,... | collective-permute-start | bytes 344072 | tf_op jit(solution)/shard_map/ppermute | solution.py:37
  179.5 26.0 %collective-permute-start.12 = (bf16[64,896]{1,0:T(8,128)(2,1)S(1)}, bf16[64,896]{1,0:T(8,128)(2,1)S(1)}, u32[]{:S(2)}, u32[]{:S(2)}) collective-permute-start(bf16[64,896]{1,0:T(8,128)(2,1)S(1)} %get-tuple-element.24), channel_id=1, source_target_pairs={{0,4},{1,5},{2,6},{3,7},{4,0},{5,1},{6,2},{7,3},{8,12},{9,13},{10,... | collective-permute-start | bytes 344072 | tf_op jit(solution)/shard_map/ppermute | solution.py:37
  189.9 11.0 %collective-permute-start.20 = (bf16[4,64,896]{2,1,0:T(8,128)(2,1)S(1)}, bf16[4,64,896]{2,1,0:T(8,128)(2,1)S(1)}, u32[]{:S(2)}, u32[]{:S(2)}) collective-permute-start(bf16[4,64,896]{2,1,0:T(8,128)(2,1)S(1)} %dynamic-slice_bitcast_fusion), channel_id=1, source_target_pairs={{0,1},{1,0},{2,3},{3,2},{4,5},{5,4},{6,7},{7,6},{8,9},{9,8},{10,11... | collective-permute-start | bytes 1376264 | tf_op jit(solution)/shard_map/ppermute | solution.py:37
  201.1 7.5 %collective-permute-start.21 = (bf16[64,896]{1,0:T(8,128)(2,1)S(1)}, bf16[64,896]{1,0:T(8,128)(2,1)S(1)}, u32[]{:S(2)}, u32[]{:S(2)}) collective-permute-start(bf16[64,896]{1,0:T(8,128)(2,1)S(1)} %get-tuple-element.19), channel_id=1, source_target_pairs={{0,2},{1,3},{2,4},{3,5},{4,6},{5,7},{6,0},{7,1},{8,10},{9,11},{10,... | collective-permute-start | bytes 344072 | tf_op jit(solution)/shard_map/ppermute | solution.py:37
  201.7 7.0 %collective-permute-start.23 = (bf16[64,896]{1,0:T(8,128)(2,1)S(1)}, bf16[64,896]{1,0:T(8,128)(2,1)S(1)}, u32[]{:S(2)}, u32[]{:S(2)}) collective-permute-start(bf16[64,896]{1,0:T(8,128)(2,1)S(1)} %get-tuple-element.20), channel_id=1, source_target_pairs={{0,6},{1,7},{2,0},{3,1},{4,2},{5,3},{6,4},{7,5},{8,14},{9,15},{10,... | collective-permute-start | bytes 344072 | tf_op jit(solution)/shard_map/ppermute | solution.py:37
  205.0 8.5 %collective-permute-start.22 = (bf16[64,896]{1,0:T(8,128)(2,1)S(1)}, bf16[64,896]{1,0:T(8,128)(2,1)S(1)}, u32[]{:S(2)}, u32[]{:S(2)}) collective-permute-start(bf16[64,896]{1,0:T(8,128)(2,1)S(1)} %get-tuple-element.21), channel_id=1, source_target_pairs={{0,4},{1,5},{2,6},{3,7},{4,0},{5,1},{6,2},{7,3},{8,12},{9,13},{10,... | collective-permute-start | bytes 344072 | tf_op jit(solution)/shard_map/ppermute | solution.py:37
  (7 other events, 21.7 us)
Sparse Core Ops, SparseCore 0:
  10.8 49.2 all-gather.2

commit v2 on v1

--- a/solution.py
+++ b/solution.py
@@ -1,6 +1,8 @@
 import jax
 import jax.numpy as jnp
 from jax import lax
+from jax.experimental import pallas as pl
+from jax.experimental.pallas import tpu as pltpu
 from jax.sharding import PartitionSpec as P
 
 EXPERTS = 32
@@ -45,18 +47,6 @@
     return lax.dynamic_index_in_dim(x, i, 0, keepdims=False)
 
 
-def dp_sum_pair(part, core, n_dp):
-    got = send(at(part, 1 - core), "dp", flip(n_dp, 1))
-    both = (at(part, core).astype(F32) + got.astype(F32)).astype(BF16)
-    far = send(both, "dp", flip(n_dp, 2))
-    return both.astype(F32) + far.astype(F32)
-
-
-def share_pair(x, core, n_dp):
-    got = send(x, "dp", flip(n_dp, 1))
-    return jnp.where(core == 0, jnp.stack([x, got]), jnp.stack([got, x]))
-
-
 def return_sum(full, n_ex):
     tok = full.shape[0] // n_ex
     n_z = n_ex // 2
@@ -73,6 +63,334 @@
     return total.astype(BF16)
 
 
+TILE = 256
+
+
+def block_tables(route, first_expert, local_count, top):
+    tok = route.shape[1]
+    rows = local_count * CAP
+    number = lax.broadcasted_iota(jnp.int32, (rows, tok), 0)
+    wanted = (first_expert + number // CAP).astype(F32)
+    named = jnp.zeros((rows, tok), F32)
+    gate = jnp.zeros((rows, tok), F32)
+    for k in range(top):
+        hit = route[k : k + 1, :] == wanted
+        named = jnp.where(hit, 1.0, named)
+        gate = jnp.where(hit, route[top + k : top + k + 1, :], gate)
+    before = lax.broadcasted_iota(jnp.int32, (tok, tok), 0)
+    after = lax.broadcasted_iota(jnp.int32, (tok, tok), 1)
+    earlier = jnp.where(before < after, 1.0, 0.0).astype(BF16)
+    rank = jnp.dot(named.astype(BF16), earlier, preferred_element_type=F32)
+    pick = jnp.where(rank == (number % CAP).astype(F32), named, 0.0)
+    return pick, pick * gate
+
+
+def front_kernel(
+    both_ref, route_ref, wg_hbm, wu_hbm, wd_hbm,
+    rows_in_out, rows_dy_out, pick_out, weighted_out, hidden_out, gate_grad_out, up_grad_out,
+    wg, wu, wd, gathered, routes, rows_in, rows_dy, pick_all, weighted_all,
+    away, own, near, far, hidden, gate_grad, up_grad,
+    load_sem, keep_sem, tok_send, tok_recv, route_send, route_recv,
+    core_send, core_recv, y_send, y_recv, share_send, share_recv, share_keep,
+):
+    count, width, ffw = wg.shape
+    n_ex, tok, _ = gathered.shape
+    n_z = n_ex // 2
+    top = route_ref.shape[0] // 2
+    dp = lax.axis_index("dp")
+    me = lax.axis_index("expert")
+    z = me // 2
+    x = me % 2
+    core = dp % 2
+    x_peer = (dp, z * 2 + 1 - x)
+    core_peer = (dp + 1 - 2 * core, me)
+    y_peer = ((dp + 2) % 4, me)
+    z_peers = [(dp, ((z + k) % n_z) * 2 + x) for k in range(1, n_z)]
+    first_expert = me * count
+
+    loads = [
+        pltpu.make_async_copy(a, b, load_sem.at[i])
+        for i, (a, b) in enumerate(((wg_hbm, wg), (wu_hbm, wu), (wd_hbm, wd)))
+    ]
+    for c in loads:
+        c.start()
+
+    barrier = pltpu.get_barrier_semaphore()
+    peers = [x_peer, core_peer, y_peer] + z_peers
+    for p in peers:
+        pl.semaphore_signal(barrier, inc=1, device_id=p, device_id_type=pl.DeviceIdType.MESH)
+    pl.semaphore_wait(barrier, len(peers))
+
+    def remote(src, dst, s, r, i, to):
+        return pltpu.make_async_remote_copy(
+            src_ref=src, dst_ref=dst, send_sem=s.at[i], recv_sem=r.at[i],
+            device_id=to, device_id_type=pl.DeviceIdType.MESH,
+        )
+
+    copies = {}
+    for name, src, dst, s, r in (
+        ("route", route_ref, routes, route_send, route_recv),
+        ("tok", both_ref, gathered, tok_send, tok_recv),
+    ):
+        for k in range(1, n_z):
+            copies[name, k] = remote(src, dst.at[me], s, r, k, z_peers[k - 1])
+        copies[name, n_z] = remote(src, dst.at[me], s, r, n_z, x_peer)
+        for k in range(1, n_z + 1):
+            copies[name, k].start()
+
+    gathered[me] = both_ref[...]
+    routes[me] = route_ref[...]
+
+    def place(b):
+        pick, weighted = block_tables(routes[b], first_expert, count, top)
+        row_gate = jnp.sum(weighted, axis=1, keepdims=True)
+        sel = pick.astype(BF16)
+        at = pl.ds(pl.multiple_of(b * CAP, CAP), CAP)
+        a = jnp.dot(sel, gathered[b, :, :width], preferred_element_type=F32).astype(BF16)
+        d = jnp.dot(sel, gathered[b, :, width:], preferred_element_type=F32) * row_gate
+        d = d.astype(BF16)
+        for e in range(count):
+            rows_in[e, at, :] = a[e * CAP : (e + 1) * CAP]
+            rows_dy[e, at, :] = d[e * CAP : (e + 1) * CAP]
+
+    place(me)
+    for k in range(1, n_z):
+        slot = ((z + n_z - k) % n_z) * 2 + x
+        for name, buf, s, r in (
+            ("route", routes, route_send, route_recv),
+            ("tok", gathered, tok_send, tok_recv),
+        ):
+            copies[name, k].wait_recv()
+            copies[name, n_z + k] = remote(buf.at[slot], buf.at[slot], s, r, n_z + k, x_peer)
+            copies[name, n_z + k].start()
+        place(slot)
+    for k in range(n_z):
+        copies["route", n_z + k].wait_recv()
+        copies["tok", n_z + k].wait_recv()
+        place(((z + n_z - k) % n_z) * 2 + 1 - x)
+
+    keeps = [
+        pltpu.make_async_copy(rows_in, rows_in_out, keep_sem.at[0]),
+        pltpu.make_async_copy(rows_dy, rows_dy_out, keep_sem.at[1]),
+    ]
+    for c in keeps:
+        c.start()
+
+    def part(kind, e, dst):
+        def tile(i, _):
+            cols = pl.ds(pl.multiple_of(i * TILE, TILE), TILE)
+            if kind == 2:
+                v = lax.dot_general(
+                    rows_dy[e], wd[e, cols, :], (((1,), (1,)), ((), ())),
+                    preferred_element_type=F32,
+                )
+            else:
+                w = wg if kind == 0 else wu
+                v = jnp.dot(rows_in[e], w[e, :, cols], preferred_element_type=F32)
+            dst[:, cols] = v.astype(BF16)
+            return 0
+
+        lax.fori_loop(0, ffw // TILE, tile, 0)
+
+    chunks = [(kind, j) for j in range(count // 2) for kind in (0, 1)]
+    chunks += [(2, j) for j in range(count // 2)]
+    core_copies, y_copies, loaded = [], [], set()
+
+    def chunk_away(i):
+        kind, j = chunks[i]
+        if kind not in loaded:
+            loads[kind].wait()
+            loaded.add(kind)
+        part(kind, 2 * j + 1 - core, away.at[i])
+        core_copies.append(remote(away.at[i], near.at[i], core_send, core_recv, i, core_peer))
+        core_copies[i].start()
+
+    rows = rows_in.shape[1]
+    step = 32
+
+    def chunk_sum(i):
+        core_copies[i].wait_recv()
+
+        def some(r, _):
+            at = pl.ds(pl.multiple_of(r * step, step), step)
+            v = own[i, at, :].astype(F32) + near[i, at, :].astype(F32)
+            own[i, at, :] = v.astype(BF16)
+            return 0
+
+        lax.fori_loop(0, rows // step, some, 0)
+        y_copies.append(remote(own.at[i], far.at[i], y_send, y_recv, i, y_peer))
+        y_copies[i].start()
+
+    for i, (kind, j) in enumerate(chunks):
+        chunk_away(i)
+        if i > 0:
+            chunk_sum(i - 1)
+        part(kind, 2 * j + core, own.at[i])
+    chunk_sum(len(chunks) - 1)
+
+    pick_all[...] = jnp.zeros_like(pick_all)
+    weighted_all[...] = jnp.zeros_like(weighted_all)
+    for b in range(n_ex):
+        pick, weighted = block_tables(routes[b], first_expert, count, top)
+        for e in range(count):
+            r = slice(e * CAP, (e + 1) * CAP)
+            o = (e, slice(b * CAP, (b + 1) * CAP), slice(b * tok, (b + 1) * tok))
+            pick_all[o] = pick[r].astype(BF16)
+            weighted_all[o] = weighted[r].astype(BF16)
+    keeps += [
+        pltpu.make_async_copy(pick_all, pick_out, keep_sem.at[2]),
+        pltpu.make_async_copy(weighted_all, weighted_out, keep_sem.at[3]),
+    ]
+    for c in keeps[2:]:
+        c.start()
+
+    shares = []
+
+    def share(src, dst, i, j):
+        e = 2 * j + core
+        shares.append(remote(src.at[j], dst.at[e], share_send, share_recv, i, core_peer))
+        shares[-1].start()
+        keeps.append(pltpu.make_async_copy(src.at[j], dst.at[e], share_keep.at[i]))
+        keeps[-1].start()
+
+    def total(i, at):
+        return own[i, at, :].astype(F32) + far[i, at, :].astype(F32)
+
+    pairs = count // 2
+    for j in range(pairs):
+        y_copies[2 * j].wait_recv()
+        y_copies[2 * j + 1].wait_recv()
+
+        def forward(r, _):
+            at = pl.ds(pl.multiple_of(r * step, step), step)
+            g = total(2 * j, at)
+            hidden[j, at, :] = (g * jax.nn.sigmoid(g) * total(2 * j + 1, at)).astype(BF16)
+            return 0
+
+        lax.fori_loop(0, rows // step, forward, 0)
+        share(hidden, hidden_out, j, j)
+    for j in range(pairs):
+        y_copies[2 * pairs + j].wait_recv()
+
+        def backward(r, _):
+            at = pl.ds(pl.multiple_of(r * step, step), step)
+            g, u, h = total(2 * j, at), total(2 * j + 1, at), total(2 * pairs + j, at)
+            logistic = jax.nn.sigmoid(g)
+            up_grad[j, at, :] = (h * g * logistic).astype(BF16)
+            gate_grad[j, at, :] = (h * u * logistic * (1.0 + g * (1.0 - logistic))).astype(BF16)
+            return 0
+
+        lax.fori_loop(0, rows // step, backward, 0)
+        share(gate_grad, gate_grad_out, pairs + 2 * j, j)
+        share(up_grad, up_grad_out, pairs + 2 * j + 1, j)
+
+    for c in copies.values():
+        c.wait_send()
+    for c in core_copies + y_copies:
+        c.wait_send()
+    for c in shares + keeps:
+        c.wait()
+
+
+def front(both, route, w_gate, w_up, w_down, n_ex):
+    count, width, ffw = w_gate.shape
+    rows = n_ex * CAP
+    tok = both.shape[0]
+    chunks = 3 * count // 2
+    pairs = count // 2
+    shape = jax.ShapeDtypeStruct
+    vmem = pl.BlockSpec(memory_space=pltpu.VMEM)
+    hbm = pl.BlockSpec(memory_space=pl.ANY)
+    dma = pltpu.SemaphoreType.DMA
+    return pl.pallas_call(
+        front_kernel,
+        out_shape=[
+            shape((count, rows, width), BF16),
+            shape((count, rows, width), BF16),
+            shape((count, rows, n_ex * tok), BF16),
+            shape((count, rows, n_ex * tok), BF16),
+            shape((count, rows, ffw), BF16),
+            shape((count, rows, ffw), BF16),
+            shape((count, rows, ffw), BF16),
+        ],
+        in_specs=[vmem, vmem, hbm, hbm, hbm],
+        out_specs=[hbm] * 7,
+        scratch_shapes=[
+            pltpu.VMEM(w_gate.shape, BF16),
+            pltpu.VMEM(w_up.shape, BF16),
+            pltpu.VMEM(w_down.shape, BF16),
+            pltpu.VMEM((n_ex,) + both.shape, BF16),
+            pltpu.VMEM((n_ex,) + route.shape, F32),
+            pltpu.VMEM((count, rows, width), BF16),
+            pltpu.VMEM((count, rows, width), BF16),
+            pltpu.VMEM((count, rows, n_ex * tok), BF16),
+            pltpu.VMEM((count, rows, n_ex * tok), BF16),
+        ]
+        + [pltpu.VMEM((chunks, rows, ffw), BF16)] * 4
+        + [pltpu.VMEM((pairs, rows, ffw), BF16)] * 3
+        + [dma((3,)), dma((4,))]
+        + [dma((n_ex,))] * 4
+        + [dma((chunks,))] * 4
+        + [dma((3 * pairs,))] * 3,
+        compiler_params=pltpu.CompilerParams(
+            collective_id=0, has_side_effects=True, vmem_limit_bytes=58 * 1024 * 1024
+        ),
+        cost_estimate=pl.CostEstimate(
+            flops=6 * count * rows * width * ffw, bytes_accessed=64 << 20, transcendentals=0
+        ),
+        name="front",
+    )(both, route, w_gate, w_up, w_down)
+
+
+def front_general(both, route, w_gate, w_up, w_down, n_ex):
+    count, width, _ = w_gate.shape
+    rows = n_ex * CAP
+    top = route.shape[1] // 2
+    route = lax.all_gather(route, "expert", axis=0, tiled=True)
+    both = lax.all_gather(both, "expert", axis=0, tiled=True)
+    pick, weighted, row_gate = tables(
+        route[:, :top].astype(jnp.int32),
+        route[:, top:],
+        lax.axis_index("expert") * count,
+        count,
+        n_ex,
+    )
+    picked = mm(pick, both)
+    rows_in = picked[:, :width].astype(BF16).reshape(count, rows, width)
+    rows_dy = (picked[:, width:] * row_gate).astype(BF16).reshape(count, rows, width)
+
+    def gate_up(e, w):
+        return mm(rows_in[e], w[e]).astype(BF16)
+
+    def back(e):
+        return mm(rows_dy[e], w_down[e], ((1,), (1,))).astype(BF16)
+
+    def forward(gate_sum, up_sum):
+        logistic = jax.nn.sigmoid(gate_sum)
+        return (gate_sum * logistic * up_sum).astype(BF16)
+
+    def backward(gate_sum, up_sum, hidden_grad):
+        logistic = jax.nn.sigmoid(gate_sum)
+        up_grad = (hidden_grad * gate_sum * logistic).astype(BF16)
+        gate_grad = (
+            hidden_grad * up_sum * logistic * (1.0 + gate_sum * (1.0 - logistic))
+        ).astype(BF16)
+        return gate_grad, up_grad
+
+    gate_sum, up_sum, hidden_grad = (
+        lax.psum(jnp.stack(p), "dp").astype(F32)
+        for p in (
+            [gate_up(e, w_gate) for e in range(count)],
+            [gate_up(e, w_up) for e in range(count)],
+            [back(e) for e in range(count)],
+        )
+    )
+    hidden = forward(gate_sum, up_sum)
+    gate_grad, up_grad = backward(gate_sum, up_sum, hidden_grad)
+
+    return rows_in, rows_dy, pick, weighted, hidden, gate_grad, up_grad
+
+
 def make_body(n_dp, n_ex):
     fast = n_dp == 4 and n_ex == 8
 
@@ -80,67 +398,18 @@
         width = tokens.shape[1]
         count = w_gate.shape[0]
         rows = n_ex * CAP
-        core = lax.axis_index("dp") % 2
+        both = jnp.concatenate([tokens, cotangent], axis=1)
         route = jnp.concatenate([expert_ids.astype(F32), gate_weights], axis=1)
-        route = lax.all_gather(route, "expert", axis=0, tiled=True)
-        top = expert_ids.shape[1]
-        both = jnp.concatenate([tokens, cotangent], axis=1)
-        both = lax.all_gather(both, "expert", axis=0, tiled=True)
-        pick, weighted, row_gate = tables(
-            route[:, :top].astype(jnp.int32),
-            route[:, top:],
-            lax.axis_index("expert") * count,
-            count,
-            n_ex,
-        )
-        picked = mm(pick, both)
-        rows_in = picked[:, :width].astype(BF16).reshape(count, rows, width)
-        rows_dy = (picked[:, width:] * row_gate).astype(BF16).reshape(count, rows, width)
-
-        def gate_up(e, w):
-            return mm(rows_in[e], w[e]).astype(BF16)
-
-        def back(e):
-            return mm(rows_dy[e], w_down[e], ((1,), (1,))).astype(BF16)
-
-        def forward(gate_sum, up_sum):
-            logistic = jax.nn.sigmoid(gate_sum)
-            return (gate_sum * logistic * up_sum).astype(BF16)
-
-        def backward(gate_sum, up_sum, hidden_grad):
-            logistic = jax.nn.sigmoid(gate_sum)
-            up_grad = (hidden_grad * gate_sum * logistic).astype(BF16)
-            gate_grad = (
-                hidden_grad * up_sum * logistic * (1.0 + gate_sum * (1.0 - logistic))
-            ).astype(BF16)
-            return gate_grad, up_grad
-
         if fast:
-            halves = range(0, count, 2)
-            sums = []
-            for e in halves:
-                g = dp_sum_pair(jnp.stack([gate_up(e, w_gate), gate_up(e + 1, w_gate)]), core, n_dp)
-                u = dp_sum_pair(jnp.stack([gate_up(e, w_up), gate_up(e + 1, w_up)]), core, n_dp)
-                sums.append((g, u))
-            grads = [dp_sum_pair(jnp.stack([back(e), back(e + 1)]), core, n_dp) for e in halves]
-            hidden = jnp.concatenate([share_pair(forward(g, u), core, n_dp) for g, u in sums])
-            pairs = [
-                share_pair(jnp.stack(backward(g, u, h)), core, n_dp)
-                for (g, u), h in zip(sums, grads)
-            ]
-            gate_grad = jnp.concatenate([p[:, 0] for p in pairs])
-            up_grad = jnp.concatenate([p[:, 1] for p in pairs])
+            rows_in, rows_dy, pick, weighted, hidden, gate_grad, up_grad = front(
+                both, route.T, w_gate, w_up, w_down, n_ex
+            )
+            pick = pick.reshape(count * rows, -1)
+            weighted = weighted.reshape(count * rows, -1)
         else:
-            gate_sum, up_sum, hidden_grad = (
-                lax.psum(jnp.stack(p), "dp").astype(F32)
-                for p in (
-                    [gate_up(e, w_gate) for e in range(count)],
-                    [gate_up(e, w_up) for e in range(count)],
-                    [back(e) for e in range(count)],
-                )
+            rows_in, rows_dy, pick, weighted, hidden, gate_grad, up_grad = front_general(
+                both, route, w_gate, w_up, w_down, n_ex
             )
-            hidden = forward(gate_sum, up_sum)
-            gate_grad, up_grad = backward(gate_sum, up_sum, hidden_grad)
 
         out_rows = jnp.concatenate([mm(hidden[e], w_down[e]).astype(BF16) for e in range(count)])
         mixed = mm(weighted, out_rows, ((0,), (0,))).astype(BF16)

time: 225 us -> 189 us (0.84); the launches traced: 221 us -> 188 us
  Pallas kernels: 0 us -> 112 us
  waiting for transfers between devices: 70.9 us -> 14.3 us
  blocking collectives: 32.5 us -> 0 us
  other arithmetic: 22.2 us -> 6.32 us
  between operations: 15.2 us -> 0.85 us
  local copies, waits for them, and re-layouts: 13 us -> 2.65 us
  matrix products: 47.5 us -> 38.1 us
  starting transfers between devices: 20.2 us -> 13.9 us
    pallas_call x0 -> x1, Pallas kernels: none -> 112 us  [front(): pl.pallas_call(front_kernel, out_shape=[shape((count, rows, width), BF16)...]
    ppermute x24 -> x8, waiting for transfers between devices: 60.4 us -> 14.3 us  [send(): return lax.ppermute(x, axis, pairs)]
    all_gather x1 -> x0, blocking collectives: 32.5 us -> none  [body(): route = lax.all_gather(route, 'expert', axis=0, tiled=True)]
    all_gather x1 -> x0, waiting for transfers between devices: 10.5 us -> none  [body(): both = lax.all_gather(both, 'expert', axis=0, tiled=True)]
    dot_general x27 -> x14, matrix products: 31.6 us -> 22 us  [mm(): return lax.dot_general(a, b, (dims, ((), ())), preferred_element_type=F32)]
    ppermute x24 -> x8, starting transfers between devices: 20.2 us -> 13.9 us  [send(): return lax.ppermute(x, axis, pairs)]
    broadcast_in_dim x3 -> x0, local copies, waits for them, and re-layouts: 5.84 us -> none  [tables(): weighted = jnp.where(pick, gate[:, None, None, :, :], 0.0)]
    convert_element_type x7 -> x0, other arithmetic: 5.8 us -> none  [the longest x6 5.52 us: dp_sum_pair(): both = (at(part, core).astype(F32) + got.astype(F32)).astype(BF16)]
  transfers between devices with their start and end apart: 25 -> 8, of which waited for: 9 -> 2; matrix products, arithmetic and copies ran while one was open for 27% -> 13% of each run, Pallas kernels for 0% -> 0%
where the time goes in v2:
time: 189 us; the launch traced here: 188 us
  Pallas kernels  112 us (59%)
  matrix products  38.1 us (20%)
  waiting for transfers between devices  14.3 us (8%)
  starting transfers between devices  13.9 us (7%)
  other arithmetic  6.32 us (3%)
  local copies, waits for them, and re-layouts  2.65 us (1%)
    pallas_call x1, Pallas kernels, front(): pl.pallas_call(front_kernel, out_shape=[shape((count, rows, width), BF16)...  112 us
    dot_general x14, matrix products, mm(): return lax.dot_general(a, b, (dims, ((), ())), preferred_element_type=F32)  22 us
    ppermute x8, waiting for transfers between devices, send(): return lax.ppermute(x, axis, pairs)  14.3 us
    ppermute x8, starting transfers between devices, send(): return lax.ppermute(x, axis, pairs)  13.9 us
    dot_general x1, matrix products, body(): jnp.einsum('erf,erd->efd', hidden, rows_dy, preferred_element_type=F32)  5.45 us
    dot_general x1, matrix products, body(): jnp.einsum('erd,erf->edf', rows_in, up_grad, preferred_element_type=F32)  5.43 us
    dot_general x1, matrix products, body(): jnp.einsum('erd,erf->edf', rows_in, gate_grad, preferred_element_type=F32)  5.19 us
  transfers between devices with their start and end apart: 8, of which 2 were waited for; matrix products, arithmetic and copies ran while one was open for 13% of the time, Pallas kernels for 0%

profile of v2, /device:TPU:0, one launch (start us, length us, event | category | flops | bytes accessed | tf_op | source)
XLA Modules:
  0.0 188.2 jit_solution(398204589545142373)
XLA Ops:
  0.6 0.7 convert_element_type.102
  1.3 1.3 maximum_bitcast_fusion.route_ref
  2.6 1.7 pad_maximum_fusion.both_ref
  4.3 112.0 %front.1 = (bf16[4,256,896]{2,1,0:T(8,128)(2,1)}, bf16[4,256,896]{2,1,0:T(8,128)(2,1)}, bf16[4,256,512]{2,1,0:T(8,128)(2,1)}, bf16[4,256,512]{2,1,0:T(8,128)(2,1...) custom-call(bf16[64,1792]{1,0:T(8,128)(2,1)} %pad_maximum_fusion.both_ref, ...), custom_call_target="tpu_custom_call" | custom-call | flops 5637144576 | bytes 67108864 | tf_op jit(solution)/shard_map/front/pallas_call | solution.py:305
  116.3 3.3 %fusion.91 = bf16[256,896]{1,0:T(8,128)(2,1)} fusion(bf16[4,1024,896]{2,1,0:T(8,128)(2,1)} %wd_hbm.1, bf16[4,256,1024]{2,1,0:T(8,128)(2,1)} %get-tuple-element.13), kind=kOutput, calls=%fused_computation.68 | convolution fusion | flops 469991424 | bytes 2818048 | tf_op jit(solution)/shard_map/dot_general | solution.py:15
  119.6 3.2 %fusion.88 = bf16[256,896]{1,0:T(8,128)(2,1)} fusion(bf16[4,1024,896]{2,1,0:T(8,128)(2,1)} %wd_hbm.1, bf16[4,256,1024]{2,1,0:T(8,128)(2,1)} %get-tuple-element.13), kind=kOutput, calls=%fused_computation.67 | convolution fusion | flops 469991424 | bytes 2818048 | tf_op jit(solution)/shard_map/dot_general | solution.py:15
  122.7 2.5 %fusion.85 = bf16[256,896]{1,0:T(8,128)(2,1)} fusion(bf16[4,1024,896]{2,1,0:T(8,128)(2,1)S(1)} %copy-done, bf16[4,256,1024]{2,1,0:T(8,128)(2,1)} %get-tuple-element.13), kind=kOutput, calls=%fused_computation.66 | convolution fusion | flops 469991424 | bytes 2818048 | tf_op jit(solution)/shard_map/dot_general | solution.py:15
  125.3 2.7 %fusion.82 = bf16[256,896]{1,0:T(8,128)(2,1)} fusion(bf16[4,1024,896]{2,1,0:T(8,128)(2,1)S(1)} %copy-done, bf16[4,256,1024]{2,1,0:T(8,128)(2,1)} %get-tuple-element.13), kind=kOutput, calls=%fused_computation.65 | convolution fusion | flops 469991424 | bytes 2818048 | tf_op jit(solution)/shard_map/dot_general | solution.py:15
  128.0 3.2 %fusion.55 = bf16[512,896]{1,0:T(8,128)(2,1)S(1)} fusion(bf16[1024,512]{1,0:T(8,128)(2,1)} %bitcast.151, bf16[256,896]{1,0:T(8,128)(2,1)} %fusion.91, bf16[256,896]{1,0:T(8,128)(2,1)} %fusion.88, bf16[256,896]{1,0:T(8,128)(2,1)} %fusion.85, bf16[256,896]{1,0:T(8,128)(2,1)} %fusion.82), kind=kOutput, calls=%fused_computation.56 | convolution fusion | flops 947322880 | bytes 3801088 | tf_op jit(solution)/shard_map/dot_general | solution.py:15
  131.1 0.9 dynamic-slice_bitcast_fusion.1
  132.1 0.7 fusion.16
  132.8 0.7 fusion.20
  133.6 0.7 fusion.24
  134.4 0.7 fusion.28
  136.2 0.7 fusion.70
  137.0 0.8 fusion.73
  137.7 0.8 fusion.76
  138.5 0.7 fusion.79
  139.7 1.3 fusion.52
  141.0 2.1 %collective-permute-start.4 = (bf16[4,64,896]{2,1,0:T(8,128)(2,1)S(1)}, bf16[4,64,896]{2,1,0:T(8,128)(2,1)S(1)}, u32[]{:S(2)}, u32[]{:S(2)}) collective-permute-start(bf16[4,64,896]{2,1,0:T(8,128)(2,1)S(1)} %dynamic-slice_bitcast_fusion), channel_id=1, source_target_pairs={{0,1},{1,0},{2,3},{3,2},{4,5},{5,4},{6,7},{7,6},{8,9},{9,8},{10,11... | collective-permute-start | bytes 1376264 | tf_op jit(solution)/shard_map/ppermute | solution.py:39
  143.1 5.2 %convolution_convert_fusion.2 = bf16[4,896,1024]{2,1,0:T(8,128)(2,1)} fusion(bf16[4,256,896]{2,1,0:T(8,128)(2,1)S(1)} %copy-done.1, bf16[4,256,1024]{2,1,0:T(8,128)(2,1)S(1)} %copy-done.4), kind=kOutput, calls=%fused_computation.2 | convolution fusion | flops 1882718208 | bytes 11272192 | tf_op jit(solution)/shard_map/erd,erf->edf/dot_general | solution.py:432
  148.3 5.4 %convolution_convert_fusion.1 = bf16[4,896,1024]{2,1,0:T(8,128)(2,1)} fusion(bf16[4,256,896]{2,1,0:T(8,128)(2,1)S(1)} %copy-done.1, bf16[4,256,1024]{2,1,0:T(8,128)(2,1)S(1)} %copy-done.3), kind=kOutput, calls=%fused_computation.1 | convolution fusion | flops 1882718208 | bytes 11272192 | tf_op jit(solution)/shard_map/erd,erf->edf/dot_general | solution.py:435
  153.8 5.4 %convolution_convert_fusion = bf16[4,1024,896]{2,1,0:T(8,128)(2,1)} fusion(bf16[4,256,1024]{2,1,0:T(8,128)(2,1)S(1)} %copy-done.2, bf16[4,256,896]{2,1,0:T(8,128)(2,1)S(1)} %copy-done.5), kind=kOutput, calls=%fused_computation | convolution fusion | flops 1882718208 | bytes 11272192 | tf_op jit(solution)/shard_map/erf,erd->efd/dot_general | solution.py:438
  159.2 1.1 fusion.95
  160.9 6.4 %collective-permute-start.3 = (bf16[64,896]{1,0:T(8,128)(2,1)S(1)}, bf16[64,896]{1,0:T(8,128)(2,1)S(1)}, u32[]{:S(2)}, u32[]{:S(2)}) collective-permute-start(bf16[64,896]{1,0:T(8,128)(2,1)S(1)} %get-tuple-element.23), channel_id=1, source_target_pairs={{0,6},{1,7},{2,0},{3,1},{4,2},{5,3},{6,4},{7,5},{8,14},{9,15},{10,... | collective-permute-start | bytes 344072 | tf_op jit(solution)/shard_map/ppermute | solution.py:39
  167.9 2.1 %collective-permute-start.5 = (bf16[64,896]{1,0:T(8,128)(2,1)S(1)}, bf16[64,896]{1,0:T(8,128)(2,1)S(1)}, u32[]{:S(2)}, u32[]{:S(2)}) collective-permute-start(bf16[64,896]{1,0:T(8,128)(2,1)S(1)} %get-tuple-element.19), channel_id=1, source_target_pairs={{0,2},{1,3},{2,4},{3,5},{4,6},{5,7},{6,0},{7,1},{8,10},{9,11},{10,... | collective-permute-start | bytes 344072 | tf_op jit(solution)/shard_map/ppermute | solution.py:39
  170.0 1.8 collective-permute-start.7
  171.8 0.7 collective-permute-start.6
  172.4 8.6 %collective-permute-done.2 = bf16[64,896]{1,0:T(8,128)(2,1)S(1)} collective-permute-done((bf16[64,896]{1,0:T(8,128)(2,1)S(1)}, bf16[64,896]{1,0:T(8,128)(2,1)S(1)}, u32[]{:S(2)}, u32[]{:S(2)}) %collective-permute-start.2) | collective-permute-done | bytes 114720 | tf_op jit(solution)/shard_map/ppermute | solution.py:39
  181.1 0.7 fusion.125
  181.8 5.7 %collective-permute-done.6 = bf16[64,896]{1,0:T(8,128)(2,1)S(1)} collective-permute-done((bf16[64,896]{1,0:T(8,128)(2,1)S(1)}, bf16[64,896]{1,0:T(8,128)(2,1)S(1)}, u32[]{:S(2)}, u32[]{:S(2)}) %collective-permute-start.6) | collective-permute-done | bytes 114720 | tf_op jit(solution)/shard_map/ppermute | solution.py:39
  187.5 0.7 fusion.122
  (41 shorter events, 2.8 us)
Async XLA Ops:
  116.3 6.5 %copy-start = (bf16[4,1024,896]{2,1,0:T(8,128)(2,1)S(1)}, bf16[4,1024,896]{2,1,0:T(8,128)(2,1)}, u32[]{:S(2)}) copy-start(bf16[4,1024,896]{2,1,0:T(8,128)(2,1)} %wd_hbm.1) | copy-start | bytes 22020100
  125.2 6.8 %slice-start = ((s8[7340032]{0:T(1024)(128)(4,1)}), s8[3145728]{0:T(1024)(128)(4,1)S(1)}, s32[]{:S(2)}) async-start(s8[7340032]{0:T(1024)(128)(4,1)} %bitcast.142), calls=%async_computation | async-start | bytes 6291456
  127.9 4.1 %slice-start.1 = ((s8[7340032]{0:T(1024)(128)(4,1)}), s8[4194304]{0:T(1024)(128)(4,1)S(1)}, s32[]{:S(2)}) async-start(s8[7340032]{0:T(1024)(128)(4,1)} %bitcast.142), calls=%async_computation.1 | async-start | bytes 8388608
  128.0 4.1 %copy-start.3 = (bf16[4,256,1024]{2,1,0:T(8,128)(2,1)S(1)}, bf16[4,256,1024]{2,1,0:T(8,128)(2,1)}, u32[]{:S(2)}) copy-start(bf16[4,256,1024]{2,1,0:T(8,128)(2,1)} %get-tuple-element.16) | copy-start | bytes 6291460
  131.1 1.7 copy-start.6
  132.0 27.2 %collective-permute-start = (bf16[4,64,896]{2,1,0:T(8,128)(2,1)}, bf16[4,64,896]{2,1,0:T(8,128)(2,1)}, u32[]{:S(2)}, u32[]{:S(2)}) collective-permute-start(bf16[4,64,896]{2,1,0:T(8,128)(2,1)} %dynamic-slice_bitcast_fusion.1), channel_id=1, source_target_pairs={{0,1},{1,0},{2,3},{3,2},{4,5},{5,4},{6,7},{7,6},{8,9},{9,8},{10,11... | collective-permute-start | bytes 1376264 | tf_op jit(solution)/shard_map/ppermute | solution.py:39
  132.1 3.0 %slice-start.2 = ((s8[7340032]{0:T(1024)(128)(4,1)}), s8[4194304]{0:T(1024)(128)(4,1)S(1)}, s32[]{:S(2)}) async-start(s8[7340032]{0:T(1024)(128)(4,1)} %bitcast.144), calls=%async_computation.2 | async-start | bytes 8388608
  133.6 2.1 %slice-start.3 = ((s8[7340032]{0:T(1024)(128)(4,1)}), s8[3145728]{0:T(1024)(128)(4,1)S(1)}, s32[]{:S(2)}) async-start(s8[7340032]{0:T(1024)(128)(4,1)} %bitcast.144), calls=%async_computation.3 | async-start | bytes 6291456
  134.3 1.9 copy-start.4
  138.5 1.2 copy-start.8
  139.7 3.4 %copy-start.1 = (bf16[4,256,896]{2,1,0:T(8,128)(2,1)S(1)}, bf16[4,256,896]{2,1,0:T(8,128)(2,1)}, u32[]{:S(2)}) copy-start(bf16[4,256,896]{2,1,0:T(8,128)(2,1)} %get-tuple-element.17) | copy-start | bytes 5505028
  141.0 26.7 %collective-permute-start.4 = (bf16[4,64,896]{2,1,0:T(8,128)(2,1)S(1)}, bf16[4,64,896]{2,1,0:T(8,128)(2,1)S(1)}, u32[]{:S(2)}, u32[]{:S(2)}) collective-permute-start(bf16[4,64,896]{2,1,0:T(8,128)(2,1)S(1)} %dynamic-slice_bitcast_fusion), channel_id=1, source_target_pairs={{0,1},{1,0},{2,3},{3,2},{4,5},{5,4},{6,7},{7,6},{8,9},{9,8},{10,11... | collective-permute-start | bytes 1376264 | tf_op jit(solution)/shard_map/ppermute | solution.py:39
  148.3 5.4 %copy-start.2 = (bf16[4,256,1024]{2,1,0:T(8,128)(2,1)S(1)}, bf16[4,256,1024]{2,1,0:T(8,128)(2,1)}, u32[]{:S(2)}) copy-start(bf16[4,256,1024]{2,1,0:T(8,128)(2,1)} %get-tuple-element.13) | copy-start | bytes 6291460
  148.3 5.4 %copy-start.5 = (bf16[4,256,896]{2,1,0:T(8,128)(2,1)S(1)}, bf16[4,256,896]{2,1,0:T(8,128)(2,1)}, u32[]{:S(2)}) copy-start(bf16[4,256,896]{2,1,0:T(8,128)(2,1)} %get-tuple-element.18) | copy-start | bytes 5505028
  153.8 5.5 %copy-start.7 = (bf16[512,896]{1,0:T(8,128)(2,1)S(1)}, bf16[512,896]{1,0:T(8,128)(2,1)}, u32[]{:S(2)}) copy-start(bf16[512,896]{1,0:T(8,128)(2,1)} %copy-done.6) | copy-start | bytes 2752516
  160.4 11.4 %collective-permute-start.1 = (bf16[64,896]{1,0:T(8,128)(2,1)S(1)}, bf16[64,896]{1,0:T(8,128)(2,1)S(1)}, u32[]{:S(2)}, u32[]{:S(2)}) collective-permute-start(bf16[64,896]{1,0:T(8,128)(2,1)S(1)} %get-tuple-element.22), channel_id=1, source_target_pairs={{0,2},{1,3},{2,4},{3,5},{4,6},{5,7},{6,0},{7,1},{8,10},{9,11},{10,... | collective-permute-start | bytes 344072 | tf_op jit(solution)/shard_map/ppermute | solution.py:39
  160.9 11.6 %collective-permute-start.3 = (bf16[64,896]{1,0:T(8,128)(2,1)S(1)}, bf16[64,896]{1,0:T(8,128)(2,1)S(1)}, u32[]{:S(2)}, u32[]{:S(2)}) collective-permute-start(bf16[64,896]{1,0:T(8,128)(2,1)S(1)} %get-tuple-element.23), channel_id=1, source_target_pairs={{0,6},{1,7},{2,0},{3,1},{4,2},{5,3},{6,4},{7,5},{8,14},{9,15},{10,... | collective-permute-start | bytes 344072 | tf_op jit(solution)/shard_map/ppermute | solution.py:39
  167.2 13.9 %collective-permute-start.2 = (bf16[64,896]{1,0:T(8,128)(2,1)S(1)}, bf16[64,896]{1,0:T(8,128)(2,1)S(1)}, u32[]{:S(2)}, u32[]{:S(2)}) collective-permute-start(bf16[64,896]{1,0:T(8,128)(2,1)S(1)} %get-tuple-element.24), channel_id=1, source_target_pairs={{0,4},{1,5},{2,6},{3,7},{4,0},{5,1},{6,2},{7,3},{8,12},{9,13},{10,... | collective-permute-start | bytes 344072 | tf_op jit(solution)/shard_map/ppermute | solution.py:39
  167.9 13.9 %collective-permute-start.5 = (bf16[64,896]{1,0:T(8,128)(2,1)S(1)}, bf16[64,896]{1,0:T(8,128)(2,1)S(1)}, u32[]{:S(2)}, u32[]{:S(2)}) collective-permute-start(bf16[64,896]{1,0:T(8,128)(2,1)S(1)} %get-tuple-element.19), channel_id=1, source_target_pairs={{0,2},{1,3},{2,4},{3,5},{4,6},{5,7},{6,0},{7,1},{8,10},{9,11},{10,... | collective-permute-start | bytes 344072 | tf_op jit(solution)/shard_map/ppermute | solution.py:39
  170.0 11.8 %collective-permute-start.7 = (bf16[64,896]{1,0:T(8,128)(2,1)S(1)}, bf16[64,896]{1,0:T(8,128)(2,1)S(1)}, u32[]{:S(2)}, u32[]{:S(2)}) collective-permute-start(bf16[64,896]{1,0:T(8,128)(2,1)S(1)} %get-tuple-element.20), channel_id=1, source_target_pairs={{0,6},{1,7},{2,0},{3,1},{4,2},{5,3},{6,4},{7,5},{8,14},{9,15},{10,... | collective-permute-start | bytes 344072 | tf_op jit(solution)/shard_map/ppermute | solution.py:39
  171.8 15.7 %collective-permute-start.6 = (bf16[64,896]{1,0:T(8,128)(2,1)S(1)}, bf16[64,896]{1,0:T(8,128)(2,1)S(1)}, u32[]{:S(2)}, u32[]{:S(2)}) collective-permute-start(bf16[64,896]{1,0:T(8,128)(2,1)S(1)} %get-tuple-element.21), channel_id=1, source_target_pairs={{0,4},{1,5},{2,6},{3,7},{4,0},{5,1},{6,2},{7,3},{8,12},{9,13},{10,... | collective-permute-start | bytes 344072 | tf_op jit(solution)/shard_map/ppermute | solution.py:39

commit v3 on v2

v3 whole, which is shorter than its diff:
```python
import jax
import jax.numpy as jnp
from jax import lax
from jax.experimental import pallas as pl
from jax.experimental.pallas import tpu as pltpu
from jax.sharding import PartitionSpec as P

EXPERTS = 32
CAP = 32
F32 = jnp.float32
BF16 = jnp.bfloat16


def mm(a, b, dims=((1,), (0,))):
    return lax.dot_general(a, b, (dims, ((), ())), preferred_element_type=F32)


def tables(ids_all, gates_all, first_expert, local_count, blocks):
    tok = ids_all.shape[0] // blocks
    mine = first_expert + jnp.arange(local_count, dtype=jnp.int32)
    hits = ids_all[None, :, :] == mine[:, None, None]
    named = jnp.any(hits, axis=2).reshape(local_count, blocks, tok)
    gate = jnp.sum(jnp.where(hits, gates_all[None], 0.0), axis=2).reshape(local_count, blocks, tok)
    earlier = jnp.triu(jnp.ones((tok, tok), BF16), 1)
    rank = jnp.einsum("ebs,st->ebt", named.astype(BF16), earlier, preferred_element_type=F32)
    slot = jnp.arange(CAP, dtype=jnp.int32)
    block = jnp.arange(blocks, dtype=jnp.int32)
    where = jnp.where(named, rank.astype(jnp.int32), -1)
    pick = (where[:, None, None, :, :] == slot[None, None, :, None, None]) & (
        block[None, :, None, None, None] == block[None, None, None, :, None]
    )
    shape = (local_count * blocks * CAP, blocks * tok)
    weighted = jnp.where(pick, gate[:, None, None, :, :], 0.0)
    row_gate = jnp.sum(weighted, axis=(3, 4)).reshape(-1, 1)
    return pick.astype(BF16).reshape(shape), weighted.astype(BF16).reshape(shape), row_gate


def send(x, axis, pairs):
    return lax.ppermute(x, axis, pairs)


def flip(size, bit):
    return [(i, i ^ bit) for i in range(size)]


def add_column(parts, n_ex):
    n_z = n_ex // 2
    got = send(parts[n_z:], "expert", flip(n_ex, 1))
    return (parts[:n_z].astype(F32) + got.astype(F32)).astype(BF16)


def add_along(col, n_ex):
    total = col[0].astype(F32)
    for k in range(1, n_ex // 2):
        to = [(i, (i - 2 * k) % n_ex) for i in range(n_ex)]
        total += send(col[k], "expert", to).astype(F32)
    return total.astype(BF16)


TILE = 256


def block_tables(route, first_expert, local_count, top):
    tok = route.shape[1]
    rows = local_count * CAP
    number = lax.broadcasted_iota(jnp.int32, (rows, tok), 0)
    wanted = (first_expert + number // CAP).astype(F32)
    named = jnp.zeros((rows, tok), F32)
    gate = jnp.zeros((rows, tok), F32)
    for k in range(top):
        hit = route[k : k + 1, :] == wanted
        named = jnp.where(hit, 1.0, named)
        gate = jnp.where(hit, route[top + k : top + k + 1, :], gate)
    before = lax.broadcasted_iota(jnp.int32, (tok, tok), 0)
    after = lax.broadcasted_iota(jnp.int32, (tok, tok), 1)
    earlier = jnp.where(before < after, 1.0, 0.0).astype(BF16)
    rank = jnp.dot(named.astype(BF16), earlier, preferred_element_type=F32)
    pick = jnp.where(rank == (number % CAP).astype(F32), named, 0.0)
    return pick, pick * gate


def groups(n_z):
    place = [0] + list(range(2, n_z + 1)) + [1] + list(range(n_z + 1, 2 * n_z))
    cut = [0, 2 * CAP, (n_z + 1) * CAP, 2 * n_z * CAP]
    return place, cut


def front_kernel(
    both_ref, route_ref, wg_hbm, wu_hbm, wd_hbm,
    mixed_ref, token_out, rows_in_out, rows_dy_out, hidden_out, gate_grad_out, up_grad_out,
    wg, wu, wd, gathered, routes, rows_in, rows_dy, picks, weights,
    away, own, near, far, hidden, gate_grad, up_grad, results, partial, token_partial, from_x, from_z,
    load_sem, keep_sem, tok_send, tok_recv, route_send, route_recv,
    core_send, core_recv, y_send, y_recv, share_send, share_recv, ret_send, ret_recv,
):
    count, width, ffw = wg.shape
    n_ex = gathered.shape[0]
    n_z = n_ex // 2
    pairs = count // 2
    top = route_ref.shape[0] // 2
    position, cut = groups(n_z)
    dp = lax.axis_index("dp")
    me = lax.axis_index("expert")
    z = me // 2
    x = me % 2
    core = dp % 2
    x_peer = (dp, z * 2 + 1 - x)
    core_peer = (dp + 1 - 2 * core, me)
    y_peer = ((dp + 2) % 4, me)
    z_peers = [(dp, ((z + k) % n_z) * 2 + x) for k in range(1, n_z)]
    first_expert = me * count

    loads = [
        pltpu.make_async_copy(a, b, load_sem.at[i])
        for i, (a, b) in enumerate(((wg_hbm, wg), (wu_hbm, wu), (wd_hbm, wd)))
    ]
    for c in loads:
        c.start()

    barrier = pltpu.get_barrier_semaphore()
    peers = [x_peer, core_peer, y_peer] + z_peers
    for p in peers:
        pl.semaphore_signal(barrier, inc=1, device_id=p, device_id_type=pl.DeviceIdType.MESH)
    pl.semaphore_wait(barrier, len(peers))

    def remote(src, dst, s, r, i, to):
        return pltpu.make_async_remote_copy(
            src_ref=src, dst_ref=dst, send_sem=s.at[i], recv_sem=r.at[i],
            device_id=to, device_id_type=pl.DeviceIdType.MESH,
        )

    copies = {}
    kinds = (
        ("route", route_ref, routes, route_send, route_recv),
        ("tok", both_ref, gathered, tok_send, tok_recv),
    )
    for name, src, dst, s, r in kinds:
        copies[name, n_z] = remote(src, dst.at[n_z], s, r, n_z, x_peer)
        copies[name, n_z].start()
        for k in range(1, n_z):
            copies[name, k] = remote(src, dst.at[k], s, r, k, z_peers[k - 1])
            copies[name, k].start()

    def place(p, route, block):
        pick, weighted = block_tables(route, first_expert, count, top)
        picks[p] = pick.astype(BF16)
        weights[p] = weighted.astype(BF16)
        row_gate = jnp.sum(weighted, axis=1, keepdims=True)
        sel = pick.astype(BF16)
        at = slice(position[p] * CAP, (position[p] + 1) * CAP)
        a = jnp.dot(sel, block[:, :width], preferred_element_type=F32).astype(BF16)
        d = jnp.dot(sel, block[:, width:], preferred_element_type=F32) * row_gate
        d = d.astype(BF16)
        for e in range(count):
            rows_in[e, at, :] = a[e * CAP : (e + 1) * CAP]
            rows_dy[e, at, :] = d[e * CAP : (e + 1) * CAP]

    def arrived(p):
        copies["route", p].wait_recv()
        copies["tok", p].wait_recv()

    def column():
        for k in range(1, n_z):
            arrived(k)
            for name, _, buf, s, r in kinds:
                c = remote(buf.at[k], buf.at[n_z + k], s, r, n_z + k, x_peer)
                copies[name, n_z + k] = c
                c.start()
        for k in range(1, n_z):
            place(k, routes[k], gathered.at[k])

    def other_column():
        for k in range(1, n_z):
            arrived(n_z + k)
            place(n_z + k, routes[n_z + k], gathered.at[n_z + k])

    keeps = []

    def keep(src, dst):
        keeps.append(pltpu.make_async_copy(src, dst, keep_sem.at[len(keeps)]))
        keeps[-1].start()

    def part(kind, e, at, dst):
        def tile(i, _):
            cols = pl.ds(pl.multiple_of(i * TILE, TILE), TILE)
            if kind == 2:
                v = lax.dot_general(
                    rows_dy[e, at, :], wd[e, cols, :], (((1,), (1,)), ((), ())),
                    preferred_element_type=F32,
                )
            else:
                w = wg if kind == 0 else wu
                v = jnp.dot(rows_in[e, at, :], w[e, :, cols], preferred_element_type=F32)
            dst[at, cols] = v.astype(BF16)
            return 0

        lax.fori_loop(0, ffw // TILE, tile, 0)

    step = 32
    spans = [slice(cut[g], cut[g + 1]) for g in range(3)]
    core_copies, y_copies, loaded = {}, {}, set()

    def send_part(chunk):
        g, kind, j = chunk
        if kind not in loaded:
            loads[kind].wait()
            loaded.add(kind)
        i = kind * pairs + j
        part(kind, 2 * j + 1 - core, spans[g], away.at[i])
        c = remote(
            away.at[i, spans[g]], near.at[i, spans[g]], core_send, core_recv,
            g * 3 * pairs + i, core_peer,
        )
        core_copies[chunk] = c
        c.start()

    def each(g, f):
        def some(r, _):
            f(pl.ds(pl.multiple_of(cut[g] + r * step, step), step))
            return 0

        lax.fori_loop(0, (cut[g + 1] - cut[g]) // step, some, 0)

    def send_sum(chunk):
        g, kind, j = chunk
        i = kind * pairs + j
        core_copies[chunk].wait_recv()

        def add(at):
            v = own[i, at, :].astype(F32) + near[i, at, :].astype(F32)
            own[i, at, :] = v.astype(BF16)

        each(g, add)
        c = remote(
            own.at[i, spans[g]], far.at[i, spans[g]], y_send, y_recv,
            g * 3 * pairs + i, y_peer,
        )
        y_copies[chunk] = c
        c.start()

    def run(chunks):
        for i, chunk in enumerate(chunks):
            g, kind, j = chunk
            send_part(chunk)
            if i > 0:
                send_sum(chunks[i - 1])
            part(kind, 2 * j + core, spans[g], own.at[kind * pairs + j])
        send_sum(chunks[-1])

    shares = {}

    def share(buf, e, g, i):
        c = remote(
            buf.at[e, spans[g]], buf.at[e, spans[g]], share_send, share_recv,
            g * 3 * pairs + i, core_peer,
        )
        shares[g, i] = c
        c.start()

    def total(kind, j, at):
        i = kind * pairs + j
        return own[i, at, :].astype(F32) + far[i, at, :].astype(F32)

    def forward(g):
        for j in range(pairs):
            e = 2 * j + core
            y_copies[g, 0, j].wait_recv()
            y_copies[g, 1, j].wait_recv()

            def some(at):
                v = total(0, j, at)
                hidden[e, at, :] = (v * jax.nn.sigmoid(v) * total(1, j, at)).astype(BF16)

            each(g, some)
            share(hidden, e, g, j)

    def backward(g):
        for j in range(pairs):
            e = 2 * j + core
            y_copies[g, 2, j].wait_recv()

            def some(at):
                v, u, h = total(0, j, at), total(1, j, at), total(2, j, at)
                s = jax.nn.sigmoid(v)
                up_grad[e, at, :] = (h * v * s).astype(BF16)
                gate_grad[e, at, :] = (h * u * s * (1.0 + v * (1.0 - s))).astype(BF16)

            each(g, some)
            share(gate_grad, e, g, pairs + j)
            share(up_grad, e, g, 2 * pairs + j)

    col_tiles = [(c, min(c + TILE, width)) for c in range(0, width, TILE)]

    def row_grads(at):
        def one(e, _):
            for a, b in col_tiles:
                dims = (((1,), (1,)), ((), ()))
                v = lax.dot_general(
                    gate_grad[e, at, :], wg[e, a:b, :], dims, preferred_element_type=F32
                ) + lax.dot_general(
                    up_grad[e, at, :], wu[e, a:b, :], dims, preferred_element_type=F32
                )
                results[e, at, a:b] = v.astype(BF16)
            return 0

        lax.fori_loop(0, count, one, 0)

    def to_tokens(tables, out):
        for p in range(n_ex):
            at = slice(position[p] * CAP, (position[p] + 1) * CAP)
            rows = jnp.concatenate([results[e, at, :] for e in range(count)], axis=0)
            v = lax.dot_general(
                tables[p], rows, (((0,), (0,)), ((), ())), preferred_element_type=F32
            )
            out[p] = v.astype(BF16)

    place(0, route_ref[...], both_ref)
    arrived(n_z)
    place(n_z, routes[n_z], gathered.at[n_z])
    every = range(pairs)
    run([(0, kind, j) for j in every for kind in (0, 1)] + [(0, 2, j) for j in every])
    column()
    run([(1, kind, j) for j in every for kind in (0, 1)])
    other_column()
    keep(rows_in, rows_in_out)
    keep(rows_dy, rows_dy_out)
    run(
        [(2, kind, j) for j in every for kind in (0, 1)]
        + [(1, 2, j) for j in every]
        + [(2, 2, j) for j in every]
    )
    forward(0)
    backward(0)
    forward(1)
    forward(2)
    for g in range(3):
        for j in every:
            shares[g, j].wait_recv()
    keep(hidden, hidden_out)

    def out_rows(e, _):
        for a, b in col_tiles:
            v = jnp.dot(hidden[e], wd[e, :, a:b], preferred_element_type=F32)
            results[e, :, a:b] = v.astype(BF16)
        return 0

    lax.fori_loop(0, count, out_rows, 0)
    to_tokens(weights, partial)
    across = remote(partial.at[n_z:], from_x, ret_send, ret_recv, 0, x_peer)
    across.start()
    backward(1)
    for g in range(2):
        for i in range(pairs, 3 * pairs):
            shares[g, i].wait_recv()
    row_grads(slice(0, cut[2]))
    across.wait_recv()
    for k in range(n_z):
        v = partial[k].astype(F32) + from_x[k].astype(F32)
        partial[k] = v.astype(BF16)
    along = []
    for k in range(1, n_z):
        along.append(
            remote(
                partial.at[k], from_z.at[k - 1], ret_send, ret_recv, k, z_peers[n_z - k - 1]
            )
        )
        along[-1].start()
    backward(2)
    for i in range(pairs, 3 * pairs):
        shares[2, i].wait_recv()
    keep(gate_grad, gate_grad_out)
    keep(up_grad, up_grad_out)
    row_grads(spans[2])
    to_tokens(picks, token_partial)
    keep(token_partial, token_out)
    v = partial[0].astype(F32)
    for k, c in enumerate(along):
        c.wait_recv()
        v += from_z[k].astype(F32)
    mixed_ref[...] = v.astype(BF16)

    for group in (copies, core_copies, y_copies, shares):
        for c in group.values():
            c.wait_send()
    for c in [across] + along:
        c.wait_send()
    for c in keeps:
        c.wait()


def front(both, route, w_gate, w_up, w_down, n_ex):
    count, width, ffw = w_gate.shape
    rows = n_ex * CAP
    tok = both.shape[0]
    pairs = count // 2
    n_z = n_ex // 2
    shape = jax.ShapeDtypeStruct
    vmem = pl.BlockSpec(memory_space=pltpu.VMEM)
    hbm = pl.BlockSpec(memory_space=pl.ANY)
    dma = pltpu.SemaphoreType.DMA
    return pl.pallas_call(
        front_kernel,
        out_shape=[
            shape((tok, width), BF16),
            shape((n_ex, tok, width), BF16),
            shape((count, rows, width), BF16),
            shape((count, rows, width), BF16),
            shape((count, rows, ffw), BF16),
            shape((count, rows, ffw), BF16),
            shape((count, rows, ffw), BF16),
        ],
        in_specs=[vmem, vmem, hbm, hbm, hbm],
        out_specs=[vmem] + [hbm] * 6,
        scratch_shapes=[
            pltpu.VMEM(w_gate.shape, BF16),
            pltpu.VMEM(w_up.shape, BF16),
            pltpu.VMEM(w_down.shape, BF16),
            pltpu.VMEM((n_ex,) + both.shape, BF16),
            pltpu.VMEM((n_ex,) + route.shape, F32),
            pltpu.VMEM((count, rows, width), BF16),
            pltpu.VMEM((count, rows, width), BF16),
            pltpu.VMEM((n_ex, count * CAP, tok), BF16),
            pltpu.VMEM((n_ex, count * CAP, tok), BF16),
        ]
        + [pltpu.VMEM((3 * pairs, rows, ffw), BF16)] * 4
        + [pltpu.VMEM((count, rows, ffw), BF16)] * 3
        + [pltpu.VMEM((count, rows, width), BF16)]
        + [pltpu.VMEM((n_ex, tok, width), BF16)] * 2
        + [pltpu.VMEM((n_z, tok, width), BF16), pltpu.VMEM((n_z - 1, tok, width), BF16)]
        + [dma((3,)), dma((6,))]
        + [dma((n_ex,))] * 4
        + [dma((9 * pairs,))] * 6
        + [dma((n_z,))] * 2,
        compiler_params=pltpu.CompilerParams(
            collective_id=0, has_side_effects=True, vmem_limit_bytes=60 * 1024 * 1024
        ),
        cost_estimate=pl.CostEstimate(
            flops=12 * count * rows * width * ffw, bytes_accessed=64 << 20, transcendentals=0
        ),
        name="front",
    )(both, route, w_gate, w_up, w_down)


def front_general(both, route, w_gate, w_up, w_down, n_ex):
    count, width, _ = w_gate.shape
    rows = n_ex * CAP
    top = route.shape[1] // 2
    route = lax.all_gather(route, "expert", axis=0, tiled=True)
    both = lax.all_gather(both, "expert", axis=0, tiled=True)
    pick, weighted, row_gate = tables(
        route[:, :top].astype(jnp.int32),
        route[:, top:],
        lax.axis_index("expert") * count,
        count,
        n_ex,
    )
    picked = mm(pick, both)
    rows_in = picked[:, :width].astype(BF16).reshape(count, rows, width)
    rows_dy = (picked[:, width:] * row_gate).astype(BF16).reshape(count, rows, width)

    def gate_up(e, w):
        return mm(rows_in[e], w[e]).astype(BF16)

    def back(e):
        return mm(rows_dy[e], w_down[e], ((1,), (1,))).astype(BF16)

    def forward(gate_sum, up_sum):
        logistic = jax.nn.sigmoid(gate_sum)
        return (gate_sum * logistic * up_sum).astype(BF16)

    def backward(gate_sum, up_sum, hidden_grad):
        logistic = jax.nn.sigmoid(gate_sum)
        up_grad = (hidden_grad * gate_sum * logistic).astype(BF16)
        gate_grad = (
            hidden_grad * up_sum * logistic * (1.0 + gate_sum * (1.0 - logistic))
        ).astype(BF16)
        return gate_grad, up_grad

    gate_sum, up_sum, hidden_grad = (
        lax.psum(jnp.stack(p), "dp").astype(F32)
        for p in (
            [gate_up(e, w_gate) for e in range(count)],
            [gate_up(e, w_up) for e in range(count)],
            [back(e) for e in range(count)],
        )
    )
    hidden = forward(gate_sum, up_sum)
    gate_grad, up_grad = backward(gate_sum, up_sum, hidden_grad)

    return rows_in, rows_dy, pick, weighted, hidden, gate_grad, up_grad


def weight_grad(a, b):
    return jnp.einsum("erm,ern->emn", a, b, preferred_element_type=F32).astype(BF16)


def make_body(n_dp, n_ex):
    fast = n_dp == 4 and n_ex == 8

    def body(tokens, expert_ids, gate_weights, w_gate, w_up, w_down, cotangent):
        count = w_gate.shape[0]
        both = jnp.concatenate([tokens, cotangent], axis=1)
        route = jnp.concatenate([expert_ids.astype(F32), gate_weights], axis=1)
        if fast:
            mixed, parts, rows_in, rows_dy, hidden, gate_grad, up_grad = front(
                both, route.T, w_gate, w_up, w_down, n_ex
            )
            grad_down = weight_grad(hidden, rows_dy)
            col = add_column(parts, n_ex)
            rows_in, col = lax.optimization_barrier((rows_in, col))
            token_grad = add_along(col, n_ex)
        else:
            rows_in, rows_dy, pick, weighted, hidden, gate_grad, up_grad = front_general(
                both, route, w_gate, w_up, w_down, n_ex
            )
            out_rows = [mm(hidden[e], w_down[e]).astype(BF16) for e in range(count)]
            row_grad = [
                (
                    mm(gate_grad[e], w_gate[e], ((1,), (1,))) + mm(up_grad[e], w_up[e], ((1,), (1,)))
                ).astype(BF16)
                for e in range(count)
            ]
            mixed = mm(weighted, jnp.concatenate(out_rows), ((0,), (0,))).astype(BF16)
            token_grad = mm(pick, jnp.concatenate(row_grad), ((0,), (0,))).astype(BF16)
            mixed, token_grad = (
                lax.psum_scatter(v, "expert", scatter_dimension=0, tiled=True)
                for v in (mixed, token_grad)
            )
            grad_down = weight_grad(hidden, rows_dy)
        grad_gate = weight_grad(rows_in, gate_grad)
        grad_up = weight_grad(rows_in, up_grad)
        return mixed, token_grad, grad_gate, grad_up, grad_down

    return body


def solution(mesh):
    placed = (
        P("expert", "dp"),
        P("expert", None),
        P("expert", None),
        P("expert", "dp", None),
        P("expert", "dp", None),
        P("expert", None, "dp"),
        P("expert", "dp"),
    )
    return jax.shard_map(
        make_body(mesh.shape["dp"], mesh.shape["expert"]),
        mesh=mesh,
        in_specs=placed,
        out_specs=(
            P("expert", "dp"),
            P("expert", "dp"),
            P("expert", "dp", None),
            P("expert", "dp", None),
            P("expert", None, "dp"),
        ),
        check_vma=False,
    )
```

time: 189 us -> 132 us (0.70)
  matrix products: 38.1 us -> 18.1 us
  Pallas kernels: 112 us -> 98.2 us
  waiting for transfers between devices: 14.3 us -> 3.2 us
  starting transfers between devices: 13.9 us -> 5.06 us
    dot_general x17 -> x3, matrix products: 38.1 us -> 18.1 us  [weight_grad(): jnp.einsum('erm,ern->emn', a, b, preferred_element_type=F32).astype(BF16)]
    pallas_call x1, Pallas kernels: 112 us -> 98.2 us  [front(): pl.pallas_call(front_kernel, out_shape=[shape((tok, width), BF16), shape(...]
    ppermute x8 -> x4, waiting for transfers between devices: 14.3 us -> 3.2 us  [send(): return lax.ppermute(x, axis, pairs)]
    ppermute x8 -> x4, starting transfers between devices: 13.9 us -> 5.06 us  [send(): return lax.ppermute(x, axis, pairs)]
  transfers between devices with their start and end apart: 8 -> 4, of which waited for: 2 -> 1; matrix products, arithmetic and copies ran while one was open for 13% -> 14% of each run, Pallas kernels for 0% -> 0%
where the time goes in v3:
time: 132 us; the launch traced here: 131 us
  Pallas kernels  98.2 us (74%)
  matrix products  18.1 us (14%)
  starting transfers between devices  5.06 us (4%)
  other arithmetic  4.47 us (3%)
  waiting for transfers between devices  3.2 us (2%)
  local copies, waits for them, and re-layouts  1.75 us (1%)
    pallas_call x1, Pallas kernels, front(): pl.pallas_call(front_kernel, out_shape=[shape((tok, width), BF16), shape(...  98.2 us
    dot_general x3, matrix products, weight_grad(): jnp.einsum('erm,ern->emn', a, b, preferred_element_type=F32).astype(BF16)  18.1 us
    ppermute x4, starting transfers between devices, send(): return lax.ppermute(x, axis, pairs)  5.06 us
    ppermute x4, waiting for transfers between devices, send(): return lax.ppermute(x, axis, pairs)  3.2 us
  transfers between devices with their start and end apart: 4, of which 1 were waited for; matrix products, arithmetic and copies ran while one was open for 14% of the time, Pallas kernels for 0%

profile of v3, /device:TPU:0, one launch (start us, length us, event | category | flops | bytes accessed | tf_op | source)
XLA Modules:
  0.0 131.5 jit_solution(4868729748960600407)
XLA Ops:
  0.6 0.7 convert_element_type.39
  1.3 1.3 maximum_bitcast_fusion.route_ref
  2.6 1.7 %pad_maximum_fusion.both_ref = bf16[64,1792]{1,0:T(8,128)(2,1)} fusion(bf16[64,896]{1,0:T(8,128)(2,1)} %param.13, bf16[64,896]{1,0:T(8,128)(2,1)} %param.7), kind=kLoop, calls=%fused_computation.4 | loop fusion | flops 458752 | bytes 458752 | tf_op jit(solution)/shard_map/concatenate | solution.py:502
  4.3 98.2 %front.1 = (bf16[64,896]{1,0:T(8,128)(2,1)}, bf16[8,64,896]{2,1,0:T(8,128)(2,1)}, bf16[4,256,896]{2,1,0:T(8,128)(2,1)}, bf16[4,256,896]{2,1,0:T(8,128)(2,1)}, bf...) custom-call(bf16[64,1792]{1,0:T(8,128)(2,1)} %pad_maximum_fusion.both_ref, ...), custom_call_target="tpu_custom_call" | custom-call | flops 11274289152 | bytes 67108864 | tf_op jit(solution)/shard_map/front/pallas_call | solution.py:401
  102.5 1.1 slice.19
  103.6 1.8 %collective-permute-start = (bf16[4,64,896]{2,1,0:T(8,128)(2,1)S(1)}, bf16[4,64,896]{2,1,0:T(8,128)(2,1)S(1)}, u32[]{:S(2)}, u32[]{:S(2)}) collective-permute-start(bf16[4,64,896]{2,1,0:T(8,128)(2,1)S(1)} %slice.19), channel_id=1, source_target_pairs={{0,1},{1,0},{2,3},{3,2},{4,5},{5,4},{6,7},{7,6},{8,9},{9,8},{10,11... | collective-permute-start | bytes 1376264 | tf_op jit(solution)/shard_map/ppermute | solution.py:39
  105.3 0.0 copy-start.3
  105.3 0.0 copy-start.2
  105.3 7.7 %convolution_convert_fusion = bf16[4,1024,896]{2,1,0:T(8,128)(2,1)} fusion(bf16[4,256,1024]{2,1,0:T(8,128)(2,1)} %get-tuple-element.21, bf16[4,256,896]{2,1,0:T(8,128)(2,1)} %get-tuple-element.22), kind=kOutput, calls=%fused_computation | convolution fusion | flops 1882718208 | bytes 11272192 | tf_op jit(solution)/shard_map/erm,ern->emn/dot_general | solution.py:494
  113.1 0.0 copy-start
  113.1 3.2 %collective-permute-done = bf16[4,64,896]{2,1,0:T(8,128)(2,1)S(1)} collective-permute-done((bf16[4,64,896]{2,1,0:T(8,128)(2,1)S(1)}, bf16[4,64,896]{2,1,0:T(8,128)(2,1)S(1)}, u32[]{:S(2)}, u32[]{:S(2)}) %collective-permute-start) | collective-permute-done | bytes 458784 | tf_op jit(solution)/shard_map/ppermute | solution.py:39
  116.3 0.0 copy-done.3
  116.3 0.1 add_convert_fusion
  116.4 0.4 collective-permute-start.1
  116.9 1.6 %collective-permute-start.3 = (bf16[64,896]{1,0:T(8,128)(2,1)S(1)}, bf16[64,896]{1,0:T(8,128)(2,1)S(1)}, u32[]{:S(2)}, u32[]{:S(2)}) collective-permute-start(bf16[64,896]{1,0:T(8,128)(2,1)S(1)} %get-tuple-element.24), channel_id=1, source_target_pairs={{0,2},{1,3},{2,4},{3,5},{4,6},{5,7},{6,0},{7,1},{8,10},{9,11},{10,... | collective-permute-start | bytes 344072 | tf_op jit(solution)/shard_map/ppermute | solution.py:39
  118.5 1.2 collective-permute-start.2
  119.7 0.0 copy-done.2
  119.7 0.0 copy-done
  119.7 0.0 copy-start.1
  119.7 5.2 %convolution_convert_fusion.1 = bf16[4,896,1024]{2,1,0:T(8,128)(2,1)} fusion(bf16[4,256,896]{2,1,0:T(8,128)(2,1)S(1)} %copy-done, bf16[4,256,1024]{2,1,0:T(8,128)(2,1)S(1)} %copy-done.2), kind=kOutput, calls=%fused_computation.1 | convolution fusion | flops 1882718208 | bytes 11272192 | tf_op jit(solution)/shard_map/erm,ern->emn/dot_general | solution.py:494
  124.9 0.0 copy-done.1
  124.9 0.0 copy-start.4
  124.9 5.2 %convolution_convert_fusion.2 = bf16[4,896,1024]{2,1,0:T(8,128)(2,1)} fusion(bf16[4,256,896]{2,1,0:T(8,128)(2,1)S(1)} %copy-done, bf16[4,256,1024]{2,1,0:T(8,128)(2,1)S(1)} %copy-done.1), kind=kOutput, calls=%fused_computation.2 | convolution fusion | flops 1882718208 | bytes 11272192 | tf_op jit(solution)/shard_map/erm,ern->emn/dot_general | solution.py:494
  130.1 0.0 collective-permute-done.1
  130.1 0.0 collective-permute-done.3
  130.1 0.0 collective-permute-done.2
  130.1 0.7 fusion.2
  130.8 0.0 copy-done.4
  130.8 0.6 copy.19
  (1 shorter events, 0.0 us)
Async XLA Ops:
  103.6 12.7 %collective-permute-start = (bf16[4,64,896]{2,1,0:T(8,128)(2,1)S(1)}, bf16[4,64,896]{2,1,0:T(8,128)(2,1)S(1)}, u32[]{:S(2)}, u32[]{:S(2)}) collective-permute-start(bf16[4,64,896]{2,1,0:T(8,128)(2,1)S(1)} %slice.19), channel_id=1, source_target_pairs={{0,1},{1,0},{2,3},{3,2},{4,5},{5,4},{6,7},{7,6},{8,9},{9,8},{10,11... | collective-permute-start | bytes 1376264 | tf_op jit(solution)/shard_map/ppermute | solution.py:39
  105.3 10.9 %copy-start.3 = (bf16[8,64,896]{2,1,0:T(8,128)(2,1)S(1)}, bf16[8,64,896]{2,1,0:T(8,128)(2,1)}, u32[]{:S(2)}) copy-start(bf16[8,64,896]{2,1,0:T(8,128)(2,1)} %get-tuple-element.16) | copy-start | bytes 2752516
  105.3 14.4 %copy-start.2 = (bf16[4,256,1024]{2,1,0:T(8,128)(2,1)S(1)}, bf16[4,256,1024]{2,1,0:T(8,128)(2,1)}, u32[]{:S(2)}) copy-start(bf16[4,256,1024]{2,1,0:T(8,128)(2,1)} %get-tuple-element.20) | copy-start | bytes 6291460
  113.1 6.7 %copy-start = (bf16[4,256,896]{2,1,0:T(8,128)(2,1)S(1)}, bf16[4,256,896]{2,1,0:T(8,128)(2,1)}, u32[]{:S(2)}) copy-start(bf16[4,256,896]{2,1,0:T(8,128)(2,1)} %get-tuple-element.18) | copy-start | bytes 5505028
  116.4 13.7 %collective-permute-start.1 = (bf16[64,896]{1,0:T(8,128)(2,1)S(1)}, bf16[64,896]{1,0:T(8,128)(2,1)S(1)}, u32[]{:S(2)}, u32[]{:S(2)}) collective-permute-start(bf16[64,896]{1,0:T(8,128)(2,1)S(1)} %get-tuple-element.23), channel_id=1, source_target_pairs={{0,6},{1,7},{2,0},{3,1},{4,2},{5,3},{6,4},{7,5},{8,14},{9,15},{10,... | collective-permute-start | bytes 344072 | tf_op jit(solution)/shard_map/ppermute | solution.py:39
  116.9 13.2 %collective-permute-start.3 = (bf16[64,896]{1,0:T(8,128)(2,1)S(1)}, bf16[64,896]{1,0:T(8,128)(2,1)S(1)}, u32[]{:S(2)}, u32[]{:S(2)}) collective-permute-start(bf16[64,896]{1,0:T(8,128)(2,1)S(1)} %get-tuple-element.24), channel_id=1, source_target_pairs={{0,2},{1,3},{2,4},{3,5},{4,6},{5,7},{6,0},{7,1},{8,10},{9,11},{10,... | collective-permute-start | bytes 344072 | tf_op jit(solution)/shard_map/ppermute | solution.py:39
  118.5 11.6 %collective-permute-start.2 = (bf16[64,896]{1,0:T(8,128)(2,1)S(1)}, bf16[64,896]{1,0:T(8,128)(2,1)S(1)}, u32[]{:S(2)}, u32[]{:S(2)}) collective-permute-start(bf16[64,896]{1,0:T(8,128)(2,1)S(1)} %get-tuple-element.25), channel_id=1, source_target_pairs={{0,4},{1,5},{2,6},{3,7},{4,0},{5,1},{6,2},{7,3},{8,12},{9,13},{10,... | collective-permute-start | bytes 344072 | tf_op jit(solution)/shard_map/ppermute | solution.py:39
  119.7 5.2 %copy-start.1 = (bf16[4,256,1024]{2,1,0:T(8,128)(2,1)S(1)}, bf16[4,256,1024]{2,1,0:T(8,128)(2,1)}, u32[]{:S(2)}) copy-start(bf16[4,256,1024]{2,1,0:T(8,128)(2,1)} %get-tuple-element.19) | copy-start | bytes 6291460
  124.9 5.9 %copy-start.4 = (bf16[64,896]{1,0:T(8,128)(2,1)S(1)}, bf16[64,896]{1,0:T(8,128)(2,1)}, u32[]{:S(2)}) copy-start(bf16[64,896]{1,0:T(8,128)(2,1)} %get-tuple-element.31) | copy-start | bytes 344068

commit v4 on v3

--- a/solution.py
+++ b/solution.py
@@ -37,16 +37,6 @@
 
 def send(x, axis, pairs):
     return lax.ppermute(x, axis, pairs)
-
-
-def flip(size, bit):
-    return [(i, i ^ bit) for i in range(size)]
-
-
-def add_column(parts, n_ex):
-    n_z = n_ex // 2
-    got = send(parts[n_z:], "expert", flip(n_ex, 1))
-    return (parts[:n_z].astype(F32) + got.astype(F32)).astype(BF16)
 
 
 def add_along(col, n_ex):
@@ -80,16 +70,16 @@
 
 
 def groups(n_z):
-    place = [0] + list(range(2, n_z + 1)) + [1] + list(range(n_z + 1, 2 * n_z))
-    cut = [0, 2 * CAP, (n_z + 1) * CAP, 2 * n_z * CAP]
-    return place, cut
+    place = [0] + list(range(n_z + 1, 2 * n_z)) + [1] + list(range(2, n_z + 1))
+    a, b, c = 2 * CAP, (n_z + 1) * CAP, 2 * n_z * CAP
+    return place, (slice(0, a), slice(b, c), slice(a, b))
 
 
 def front_kernel(
-    both_ref, route_ref, wg_hbm, wu_hbm, wd_hbm,
+    tokens_ref, cot_ref, ids_ref, gates_ref, wg_hbm, wu_hbm, wd_hbm,
     mixed_ref, token_out, rows_in_out, rows_dy_out, hidden_out, gate_grad_out, up_grad_out,
     wg, wu, wd, gathered, routes, rows_in, rows_dy, picks, weights,
-    away, own, near, far, hidden, gate_grad, up_grad, results, partial, token_partial, from_x, from_z,
+    away, own, near, far, hidden, gate_grad, up_grad, results, partial, token_partial, from_x, from_z, token_x,
     load_sem, keep_sem, tok_send, tok_recv, route_send, route_recv,
     core_send, core_recv, y_send, y_recv, share_send, share_recv, ret_send, ret_recv,
 ):
@@ -97,8 +87,8 @@
     n_ex = gathered.shape[0]
     n_z = n_ex // 2
     pairs = count // 2
-    top = route_ref.shape[0] // 2
-    position, cut = groups(n_z)
+    top = ids_ref.shape[0]
+    position, spans = groups(n_z)
     dp = lax.axis_index("dp")
     me = lax.axis_index("expert")
     z = me // 2
@@ -117,6 +107,11 @@
     for c in loads:
         c.start()
 
+    gathered[0, :, :width] = tokens_ref[...]
+    gathered[0, :, width:] = cot_ref[...]
+    routes[0, :top, :] = ids_ref[...].astype(F32)
+    routes[0, top:, :] = gates_ref[...]
+
     barrier = pltpu.get_barrier_semaphore()
     peers = [x_peer, core_peer, y_peer] + z_peers
     for p in peers:
@@ -131,18 +126,19 @@
 
     copies = {}
     kinds = (
-        ("route", route_ref, routes, route_send, route_recv),
-        ("tok", both_ref, gathered, tok_send, tok_recv),
-    )
-    for name, src, dst, s, r in kinds:
-        copies[name, n_z] = remote(src, dst.at[n_z], s, r, n_z, x_peer)
+        ("route", routes, route_send, route_recv),
+        ("tok", gathered, tok_send, tok_recv),
+    )
+    for name, buf, s, r in kinds:
+        copies[name, n_z] = remote(buf.at[0], buf.at[n_z], s, r, n_z, x_peer)
         copies[name, n_z].start()
         for k in range(1, n_z):
-            copies[name, k] = remote(src, dst.at[k], s, r, k, z_peers[k - 1])
+            copies[name, k] = remote(buf.at[0], buf.at[k], s, r, k, z_peers[k - 1])
             copies[name, k].start()
 
-    def place(p, route, block):
-        pick, weighted = block_tables(route, first_expert, count, top)
+    def place(p):
+        block = gathered.at[p]
+        pick, weighted = block_tables(routes[p], first_expert, count, top)
         picks[p] = pick.astype(BF16)
         weights[p] = weighted.astype(BF16)
         row_gate = jnp.sum(weighted, axis=1, keepdims=True)
@@ -162,17 +158,16 @@
     def column():
         for k in range(1, n_z):
             arrived(k)
-            for name, _, buf, s, r in kinds:
+            for name, buf, s, r in kinds:
                 c = remote(buf.at[k], buf.at[n_z + k], s, r, n_z + k, x_peer)
                 copies[name, n_z + k] = c
                 c.start()
-        for k in range(1, n_z):
-            place(k, routes[k], gathered.at[k])
+            place(k)
 
     def other_column():
         for k in range(1, n_z):
             arrived(n_z + k)
-            place(n_z + k, routes[n_z + k], gathered.at[n_z + k])
+            place(n_z + k)
 
     keeps = []
 
@@ -197,7 +192,6 @@
         lax.fori_loop(0, ffw // TILE, tile, 0)
 
     step = 32
-    spans = [slice(cut[g], cut[g + 1]) for g in range(3)]
     core_copies, y_copies, loaded = {}, {}, set()
 
     def send_part(chunk):
@@ -216,10 +210,10 @@
 
     def each(g, f):
         def some(r, _):
-            f(pl.ds(pl.multiple_of(cut[g] + r * step, step), step))
+            f(pl.ds(pl.multiple_of(spans[g].start + r * step, step), step))
             return 0
 
-        lax.fori_loop(0, (cut[g + 1] - cut[g]) // step, some, 0)
+        lax.fori_loop(0, (spans[g].stop - spans[g].start) // step, some, 0)
 
     def send_sum(chunk):
         g, kind, j = chunk
@@ -305,8 +299,8 @@
 
         lax.fori_loop(0, count, one, 0)
 
-    def to_tokens(tables, out):
-        for p in range(n_ex):
+    def to_tokens(tables, out, slots):
+        for p in slots:
             at = slice(position[p] * CAP, (position[p] + 1) * CAP)
             rows = jnp.concatenate([results[e, at, :] for e in range(count)], axis=0)
             v = lax.dot_general(
@@ -314,9 +308,9 @@
             )
             out[p] = v.astype(BF16)
 
-    place(0, route_ref[...], both_ref)
+    place(0)
     arrived(n_z)
-    place(n_z, routes[n_z], gathered.at[n_z])
+    place(n_z)
     every = range(pairs)
     run([(0, kind, j) for j in every for kind in (0, 1)] + [(0, 2, j) for j in every])
     column()
@@ -326,8 +320,8 @@
     keep(rows_dy, rows_dy_out)
     run(
         [(2, kind, j) for j in every for kind in (0, 1)]
+        + [(2, 2, j) for j in every]
         + [(1, 2, j) for j in every]
-        + [(2, 2, j) for j in every]
     )
     forward(0)
     backward(0)
@@ -345,18 +339,24 @@
         return 0
 
     lax.fori_loop(0, count, out_rows, 0)
-    to_tokens(weights, partial)
+    to_tokens(weights, partial, range(n_ex))
     across = remote(partial.at[n_z:], from_x, ret_send, ret_recv, 0, x_peer)
     across.start()
-    backward(1)
-    for g in range(2):
+    backward(2)
+    for g in (0, 2):
         for i in range(pairs, 3 * pairs):
             shares[g, i].wait_recv()
-    row_grads(slice(0, cut[2]))
+    row_grads(slice(0, spans[2].stop))
+    to_tokens(picks, token_partial, range(n_z, n_ex))
+    token_across = remote(token_partial.at[n_z:], token_x, ret_send, ret_recv, n_z, x_peer)
+    token_across.start()
+
+    def add_x(mine, other):
+        for k in range(n_z):
+            mine[k] = (mine[k].astype(F32) + other[k].astype(F32)).astype(BF16)
+
     across.wait_recv()
-    for k in range(n_z):
-        v = partial[k].astype(F32) + from_x[k].astype(F32)
-        partial[k] = v.astype(BF16)
+    add_x(partial, from_x)
     along = []
     for k in range(1, n_z):
         along.append(
@@ -365,14 +365,16 @@
             )
         )
         along[-1].start()
-    backward(2)
+    backward(1)
     for i in range(pairs, 3 * pairs):
-        shares[2, i].wait_recv()
+        shares[1, i].wait_recv()
     keep(gate_grad, gate_grad_out)
     keep(up_grad, up_grad_out)
-    row_grads(spans[2])
-    to_tokens(picks, token_partial)
-    keep(token_partial, token_out)
+    row_grads(spans[1])
+    to_tokens(picks, token_partial, range(n_z))
+    token_across.wait_recv()
+    add_x(token_partial, token_x)
+    keep(token_partial.at[:n_z], token_out)
     v = partial[0].astype(F32)
     for k, c in enumerate(along):
         c.wait_recv()
@@ -382,16 +384,16 @@
     for group in (copies, core_copies, y_copies, shares):
         for c in group.values():
             c.wait_send()
-    for c in [across] + along:
+    for c in [across, token_across] + along:
         c.wait_send()
     for c in keeps:
         c.wait()
 
 
-def front(both, route, w_gate, w_up, w_down, n_ex):
+def front(tokens, cotangent, ids, gates, w_gate, w_up, w_down, n_ex):
     count, width, ffw = w_gate.shape
     rows = n_ex * CAP
-    tok = both.shape[0]
+    tok = tokens.shape[0]
     pairs = count // 2
     n_z = n_ex // 2
     shape = jax.ShapeDtypeStruct
@@ -402,21 +404,21 @@
         front_kernel,
         out_shape=[
             shape((tok, width), BF16),
-            shape((n_ex, tok, width), BF16),
+            shape((n_z, tok, width), BF16),
             shape((count, rows, width), BF16),
             shape((count, rows, width), BF16),
             shape((count, rows, ffw), BF16),
             shape((count, rows, ffw), BF16),
             shape((count, rows, ffw), BF16),
         ],
-        in_specs=[vmem, vmem, hbm, hbm, hbm],
+        in_specs=[vmem] * 4 + [hbm] * 3,
         out_specs=[vmem] + [hbm] * 6,
         scratch_shapes=[
             pltpu.VMEM(w_gate.shape, BF16),
             pltpu.VMEM(w_up.shape, BF16),
             pltpu.VMEM(w_down.shape, BF16),
-            pltpu.VMEM((n_ex,) + both.shape, BF16),
-            pltpu.VMEM((n_ex,) + route.shape, F32),
+            pltpu.VMEM((n_ex, tok, 2 * width), BF16),
+            pltpu.VMEM((n_ex, 2 * ids.shape[0], tok), F32),
             pltpu.VMEM((count, rows, width), BF16),
             pltpu.VMEM((count, rows, width), BF16),
             pltpu.VMEM((n_ex, count * CAP, tok), BF16),
@@ -427,10 +429,11 @@
         + [pltpu.VMEM((count, rows, width), BF16)]
         + [pltpu.VMEM((n_ex, tok, width), BF16)] * 2
         + [pltpu.VMEM((n_z, tok, width), BF16), pltpu.VMEM((n_z - 1, tok, width), BF16)]
+        + [pltpu.VMEM((n_z, tok, width), BF16)]
         + [dma((3,)), dma((6,))]
         + [dma((n_ex,))] * 4
         + [dma((9 * pairs,))] * 6
-        + [dma((n_z,))] * 2,
+        + [dma((n_z + 1,))] * 2,
         compiler_params=pltpu.CompilerParams(
             collective_id=0, has_side_effects=True, vmem_limit_bytes=60 * 1024 * 1024
         ),
@@ -438,7 +441,7 @@
             flops=12 * count * rows * width * ffw, bytes_accessed=64 << 20, transcendentals=0
         ),
         name="front",
-    )(both, route, w_gate, w_up, w_down)
+    )(tokens, cotangent, ids, gates, w_gate, w_up, w_down)
 
 
 def front_general(both, route, w_gate, w_up, w_down, n_ex):
@@ -499,17 +502,14 @@
 
     def body(tokens, expert_ids, gate_weights, w_gate, w_up, w_down, cotangent):
         count = w_gate.shape[0]
-        both = jnp.concatenate([tokens, cotangent], axis=1)
-        route = jnp.concatenate([expert_ids.astype(F32), gate_weights], axis=1)
         if fast:
-            mixed, parts, rows_in, rows_dy, hidden, gate_grad, up_grad = front(
-                both, route.T, w_gate, w_up, w_down, n_ex
+            mixed, col, rows_in, rows_dy, hidden, gate_grad, up_grad = front(
+                tokens, cotangent, expert_ids.T, gate_weights.T, w_gate, w_up, w_down, n_ex
             )
-            grad_down = weight_grad(hidden, rows_dy)
-            col = add_column(parts, n_ex)
-            rows_in, col = lax.optimization_barrier((rows_in, col))
             token_grad = add_along(col, n_ex)
         else:
+            both = jnp.concatenate([tokens, cotangent], axis=1)
+            route = jnp.concatenate([expert_ids.astype(F32), gate_weights], axis=1)
             rows_in, rows_dy, pick, weighted, hidden, gate_grad, up_grad = front_general(
                 both, route, w_gate, w_up, w_down, n_ex
             )
@@ -526,7 +526,7 @@
                 lax.psum_scatter(v, "expert", scatter_dimension=0, tiled=True)
                 for v in (mixed, token_grad)
             )
-            grad_down = weight_grad(hidden, rows_dy)
+        grad_down = weight_grad(hidden, rows_dy)
         grad_gate = weight_grad(rows_in, gate_grad)
         grad_up = weight_grad(rows_in, up_grad)
         return mixed, token_grad, grad_gate, grad_up, grad_down

time: 132 us -> 124 us (0.939)
  waiting for transfers between devices: 3.2 us -> 0.01 us
  other arithmetic: 4.47 us -> 1.61 us
  starting transfers between devices: 5.06 us -> 3.58 us
    ppermute x4 -> x3, waiting for transfers between devices: 3.2 us -> 0.01 us  [send(): return lax.ppermute(x, axis, pairs)]
    concatenate x1 -> x0, other arithmetic: 1.66 us -> none  [body(): both = jnp.concatenate([tokens, cotangent], axis=1)]
    ppermute x4 -> x3, starting transfers between devices: 5.06 us -> 3.58 us  [send(): return lax.ppermute(x, axis, pairs)]
  transfers between devices with their start and end apart: 4 -> 3, of which waited for: 1 -> 0; matrix products, arithmetic and copies ran while one was open for 14% -> 15% of each run, Pallas kernels for 0% -> 0%
where the time goes in v4:
time: 124 us
  Pallas kernels  98 us (79%)
  matrix products  18.1 us (15%)
  starting transfers between devices  3.58 us (3%)
  local copies, waits for them, and re-layouts  1.7 us (1%)
  other arithmetic  1.61 us (1%)
    pallas_call x1, Pallas kernels, front(): pl.pallas_call(front_kernel, out_shape=[shape((tok, width), BF16), shape(...  98 us
    dot_general x3, matrix products, weight_grad(): jnp.einsum('erm,ern->emn', a, b, preferred_element_type=F32).astype(BF16)  18.1 us
    ppermute x3, starting transfers between devices, send(): return lax.ppermute(x, axis, pairs)  3.58 us
  transfers between devices with their start and end apart: 3, of which 0 were waited for; matrix products, arithmetic and copies ran while one was open for 15% of the time, Pallas kernels for 0%

profile of v4, /device:TPU:0, one launch (start us, length us, event | category | flops | bytes accessed | tf_op | source)
XLA Modules:
  0.0 123.7 jit_solution(7652917319131500739)
XLA Ops:
  0.6 98.0 %front.1 = (bf16[64,896]{1,0:T(8,128)(2,1)}, bf16[4,64,896]{2,1,0:T(8,128)(2,1)}, bf16[4,256,896]{2,1,0:T(8,128)(2,1)}, bf16[4,256,896]{2,1,0:T(8,128)(2,1)}, bf...) custom-call(bf16[64,896]{1,0:T(8,128)(2,1)} %tokens_ref.1, ...), custom_call_target="tpu_custom_call" | custom-call | flops 11274289152 | bytes 67108864 | tf_op jit(solution)/shard_map/front/pallas_call | solution.py:403
  98.6 1.0 slice_bitcast_fusion.2
  99.7 1.5 %collective-permute-start = (bf16[64,896]{1,0:T(8,128)(2,1)S(1)}, bf16[64,896]{1,0:T(8,128)(2,1)S(1)}, u32[]{:S(2)}, u32[]{:S(2)}) collective-permute-start(bf16[64,896]{1,0:T(8,128)(2,1)S(1)} %get-tuple-element.19), channel_id=1, source_target_pairs={{0,6},{1,7},{2,0},{3,1},{4,2},{5,3},{6,4},{7,5},{8,14},{9,15},{10,... | collective-permute-start | bytes 344072 | tf_op jit(solution)/shard_map/ppermute | solution.py:39
  101.2 0.6 collective-permute-start.2
  101.8 1.5 %collective-permute-start.1 = (bf16[64,896]{1,0:T(8,128)(2,1)S(1)}, bf16[64,896]{1,0:T(8,128)(2,1)S(1)}, u32[]{:S(2)}, u32[]{:S(2)}) collective-permute-start(bf16[64,896]{1,0:T(8,128)(2,1)S(1)} %get-tuple-element.21), channel_id=1, source_target_pairs={{0,4},{1,5},{2,6},{3,7},{4,0},{5,1},{6,2},{7,3},{8,12},{9,13},{10,... | collective-permute-start | bytes 344072 | tf_op jit(solution)/shard_map/ppermute | solution.py:39
  103.3 0.0 copy-start
  103.3 0.0 copy-start.2
  103.3 7.5 %convolution_convert_fusion.2 = bf16[4,896,1024]{2,1,0:T(8,128)(2,1)} fusion(bf16[4,256,896]{2,1,0:T(8,128)(2,1)} %get-tuple-element.14, bf16[4,256,1024]{2,1,0:T(8,128)(2,1)} %get-tuple-element.15), kind=kOutput, calls=%fused_computation.2 | convolution fusion | flops 1882718208 | bytes 11272192 | tf_op jit(solution)/shard_map/erm,ern->emn/dot_general | solution.py:497
  110.7 0.0 copy-done
  110.7 0.0 copy-done.2
  110.7 0.0 copy-start.1
  110.7 0.0 copy-start.3
  110.7 5.2 %convolution_convert_fusion.1 = bf16[4,896,1024]{2,1,0:T(8,128)(2,1)} fusion(bf16[4,256,896]{2,1,0:T(8,128)(2,1)S(1)} %copy-done, bf16[4,256,1024]{2,1,0:T(8,128)(2,1)S(1)} %copy-done.2), kind=kOutput, calls=%fused_computation.1 | convolution fusion | flops 1882718208 | bytes 11272192 | tf_op jit(solution)/shard_map/erm,ern->emn/dot_general | solution.py:497
  115.9 0.0 copy-done.1
  115.9 0.0 copy-done.3
  115.9 0.0 copy-start.4
  115.9 5.4 %convolution_convert_fusion = bf16[4,1024,896]{2,1,0:T(8,128)(2,1)} fusion(bf16[4,256,1024]{2,1,0:T(8,128)(2,1)S(1)} %copy-done.1, bf16[4,256,896]{2,1,0:T(8,128)(2,1)S(1)} %copy-done.3), kind=kOutput, calls=%fused_computation | convolution fusion | flops 1882718208 | bytes 11272192 | tf_op jit(solution)/shard_map/erm,ern->emn/dot_general | solution.py:497
  121.4 0.0 collective-permute-done
  121.4 0.0 collective-permute-done.2
  121.4 0.0 collective-permute-done.1
  121.4 1.6 %fusion.2 = bf16[64,896]{1,0:T(8,128)(2,1)} fusion(bf16[64,896]{1,0:T(8,128)(2,1)S(1)} %collective-permute-done.2, bf16[64,896]{1,0:T(8,128)(2,1)S(1)} %collective-permute-done.1, bf16[64,896]{1,0:T(8,128)(2,1)S(1)} %collective-permute-done, bf16[4,64,896]{2,1,0:T(8,128)(2,1)} %get-tuple-element.13), kind=kLoop, calls=%fused_computation.6 | loop fusion | flops 458752 | bytes 573440 | tf_op jit(solution)/shard_map/convert_element_type | solution.py:47
  123.0 0.0 copy-done.4
  123.0 0.6 copy.19
Async XLA Ops:
  99.7 21.7 %collective-permute-start = (bf16[64,896]{1,0:T(8,128)(2,1)S(1)}, bf16[64,896]{1,0:T(8,128)(2,1)S(1)}, u32[]{:S(2)}, u32[]{:S(2)}) collective-permute-start(bf16[64,896]{1,0:T(8,128)(2,1)S(1)} %get-tuple-element.19), channel_id=1, source_target_pairs={{0,6},{1,7},{2,0},{3,1},{4,2},{5,3},{6,4},{7,5},{8,14},{9,15},{10,... | collective-permute-start | bytes 344072 | tf_op jit(solution)/shard_map/ppermute | solution.py:39
  101.2 20.2 %collective-permute-start.2 = (bf16[64,896]{1,0:T(8,128)(2,1)S(1)}, bf16[64,896]{1,0:T(8,128)(2,1)S(1)}, u32[]{:S(2)}, u32[]{:S(2)}) collective-permute-start(bf16[64,896]{1,0:T(8,128)(2,1)S(1)} %get-tuple-element.20), channel_id=1, source_target_pairs={{0,2},{1,3},{2,4},{3,5},{4,6},{5,7},{6,0},{7,1},{8,10},{9,11},{10,... | collective-permute-start | bytes 344072 | tf_op jit(solution)/shard_map/ppermute | solution.py:39
  101.8 19.6 %collective-permute-start.1 = (bf16[64,896]{1,0:T(8,128)(2,1)S(1)}, bf16[64,896]{1,0:T(8,128)(2,1)S(1)}, u32[]{:S(2)}, u32[]{:S(2)}) collective-permute-start(bf16[64,896]{1,0:T(8,128)(2,1)S(1)} %get-tuple-element.21), channel_id=1, source_target_pairs={{0,4},{1,5},{2,6},{3,7},{4,0},{5,1},{6,2},{7,3},{8,12},{9,13},{10,... | collective-permute-start | bytes 344072 | tf_op jit(solution)/shard_map/ppermute | solution.py:39
  103.3 7.5 %copy-start = (bf16[4,256,896]{2,1,0:T(8,128)(2,1)S(1)}, bf16[4,256,896]{2,1,0:T(8,128)(2,1)}, u32[]{:S(2)}) copy-start(bf16[4,256,896]{2,1,0:T(8,128)(2,1)} %get-tuple-element.14) | copy-start | bytes 5505028
  103.3 7.5 %copy-start.2 = (bf16[4,256,1024]{2,1,0:T(8,128)(2,1)S(1)}, bf16[4,256,1024]{2,1,0:T(8,128)(2,1)}, u32[]{:S(2)}) copy-start(bf16[4,256,1024]{2,1,0:T(8,128)(2,1)} %get-tuple-element.16) | copy-start | bytes 6291460
  110.7 5.2 %copy-start.1 = (bf16[4,256,1024]{2,1,0:T(8,128)(2,1)S(1)}, bf16[4,256,1024]{2,1,0:T(8,128)(2,1)}, u32[]{:S(2)}) copy-start(bf16[4,256,1024]{2,1,0:T(8,128)(2,1)} %get-tuple-element.17) | copy-start | bytes 6291460
  110.7 5.2 %copy-start.3 = (bf16[4,256,896]{2,1,0:T(8,128)(2,1)S(1)}, bf16[4,256,896]{2,1,0:T(8,128)(2,1)}, u32[]{:S(2)}) copy-start(bf16[4,256,896]{2,1,0:T(8,128)(2,1)} %get-tuple-element.18) | copy-start | bytes 5505028
  115.9 7.1 %copy-start.4 = (bf16[64,896]{1,0:T(8,128)(2,1)S(1)}, bf16[64,896]{1,0:T(8,128)(2,1)}, u32[]{:S(2)}) copy-start(bf16[64,896]{1,0:T(8,128)(2,1)} %get-tuple-element.27) | copy-start | bytes 344068

commit v5 on v4

--- a/solution.py
+++ b/solution.py
@@ -497,6 +497,54 @@
     return jnp.einsum("erm,ern->emn", a, b, preferred_element_type=F32).astype(BF16)
 
 
+def weights_kernel(x_ref, dy_ref, gate_ref, up_ref, hidden_ref, gate_out, up_out, down_out, xt):
+    width = x_ref.shape[2]
+    part = gate_ref.shape[2]
+
+    @pl.when(pl.program_id(1) == 0)
+    def _():
+        xt[...] = x_ref[0].T
+
+    for ref, out in ((gate_ref, gate_out), (up_ref, up_out)):
+        for c in range(0, part, TILE):
+            at = slice(c, c + TILE)
+            v = jnp.dot(xt[...], ref[0, :, at], preferred_element_type=F32)
+            out[0, :, at] = v.astype(BF16)
+    ht = hidden_ref[0].T
+    for c in range(0, width, TILE):
+        at = slice(c, min(c + TILE, width))
+        v = jnp.dot(ht, dy_ref[0, :, at], preferred_element_type=F32)
+        down_out[0, :, at] = v.astype(BF16)
+
+
+def weight_grads(rows_in, rows_dy, gate_grad, up_grad, hidden):
+    count, rows, width = rows_in.shape
+    ffw = hidden.shape[2]
+    part = ffw // 2
+    wide = pl.BlockSpec((1, rows, width), lambda e, n: (e, 0, 0))
+    some = pl.BlockSpec((1, rows, part), lambda e, n: (e, 0, n))
+    out = pl.BlockSpec((1, width, part), lambda e, n: (e, 0, n))
+    down = pl.BlockSpec((1, part, width), lambda e, n: (e, n, 0))
+    shape = jax.ShapeDtypeStruct
+    return pl.pallas_call(
+        weights_kernel,
+        grid=(count, 2),
+        out_shape=[
+            shape((count, width, ffw), BF16),
+            shape((count, width, ffw), BF16),
+            shape((count, ffw, width), BF16),
+        ],
+        in_specs=[wide, wide, some, some, some],
+        out_specs=[out, out, down],
+        scratch_shapes=[pltpu.VMEM((width, rows), BF16)],
+        compiler_params=pltpu.CompilerParams(vmem_limit_bytes=60 * 1024 * 1024),
+        cost_estimate=pl.CostEstimate(
+            flops=6 * count * rows * width * ffw, bytes_accessed=32 << 20, transcendentals=0
+        ),
+        name="weight_grads",
+    )(rows_in, rows_dy, gate_grad, up_grad, hidden)
+
+
 def make_body(n_dp, n_ex):
     fast = n_dp == 4 and n_ex == 8
 
@@ -507,6 +555,9 @@
                 tokens, cotangent, expert_ids.T, gate_weights.T, w_gate, w_up, w_down, n_ex
             )
             token_grad = add_along(col, n_ex)
+            grad_gate, grad_up, grad_down = weight_grads(
+                rows_in, rows_dy, gate_grad, up_grad, hidden
+            )
         else:
             both = jnp.concatenate([tokens, cotangent], axis=1)
             route = jnp.concatenate([expert_ids.astype(F32), gate_weights], axis=1)
@@ -526,9 +577,9 @@
                 lax.psum_scatter(v, "expert", scatter_dimension=0, tiled=True)
                 for v in (mixed, token_grad)
             )
-        grad_down = weight_grad(hidden, rows_dy)
-        grad_gate = weight_grad(rows_in, gate_grad)
-        grad_up = weight_grad(rows_in, up_grad)
+            grad_down = weight_grad(hidden, rows_dy)
+            grad_gate = weight_grad(rows_in, gate_grad)
+            grad_up = weight_grad(rows_in, up_grad)
         return mixed, token_grad, grad_gate, grad_up, grad_down
 
     return body

time: 124 us -> 122 us (0.984)
  matrix products: 18.1 us -> 0 us
  Pallas kernels: 98 us -> 114 us
    dot_general x3 -> x0, matrix products: 18.1 us -> none  [weight_grad(): jnp.einsum('erm,ern->emn', a, b, preferred_element_type=F32).astype(BF16)]
    pallas_call x0 -> x1, Pallas kernels: none -> 16 us  [weight_grads(): pl.pallas_call(weights_kernel, grid=(count, 2), out_shape=[shape((count,...]
  transfers between devices with their start and end apart: 3 -> 3, of which waited for: 0 -> 0; matrix products, arithmetic and copies ran while one was open for 15% -> 0% of each run, Pallas kernels for 0% -> 13%
where the time goes in v5:
time: 122 us
  Pallas kernels  114 us (93%)
  starting transfers between devices  3.57 us (3%)
  local copies, waits for them, and re-layouts  1.69 us (1%)
  other arithmetic  1.61 us (1%)
    pallas_call x1, Pallas kernels, front(): pl.pallas_call(front_kernel, out_shape=[shape((tok, width), BF16), shape(...  98 us
    pallas_call x1, Pallas kernels, weight_grads(): pl.pallas_call(weights_kernel, grid=(count, 2), out_shape=[shape((count,...  16 us
    ppermute x3, starting transfers between devices, send(): return lax.ppermute(x, axis, pairs)  3.57 us
  transfers between devices with their start and end apart: 3, of which 0 were waited for; matrix products, arithmetic and copies ran while one was open for 0% of the time, Pallas kernels for 13%

profile of v5, /device:TPU:0, one launch (start us, length us, event | category | flops | bytes accessed | tf_op | source)
XLA Modules:
  0.0 121.6 jit_solution(545793811348623086)
XLA Ops:
  0.6 98.0 %front.1 = (bf16[64,896]{1,0:T(8,128)(2,1)}, bf16[4,64,896]{2,1,0:T(8,128)(2,1)}, bf16[4,256,896]{2,1,0:T(8,128)(2,1)}, bf16[4,256,896]{2,1,0:T(8,128)(2,1)}, bf...) custom-call(bf16[64,896]{1,0:T(8,128)(2,1)} %tokens_ref.1, ...), custom_call_target="tpu_custom_call" | custom-call | flops 11274289152 | bytes 67108864 | tf_op jit(solution)/shard_map/front/pallas_call | solution.py:403
  98.7 1.0 slice_bitcast_fusion.2
  99.7 1.5 %collective-permute-start = (bf16[64,896]{1,0:T(8,128)(2,1)S(1)}, bf16[64,896]{1,0:T(8,128)(2,1)S(1)}, u32[]{:S(2)}, u32[]{:S(2)}) collective-permute-start(bf16[64,896]{1,0:T(8,128)(2,1)S(1)} %get-tuple-element.25), channel_id=1, source_target_pairs={{0,6},{1,7},{2,0},{3,1},{4,2},{5,3},{6,4},{7,5},{8,14},{9,15},{10,... | collective-permute-start | bytes 344072 | tf_op jit(solution)/shard_map/ppermute | solution.py:39
  101.2 0.6 collective-permute-start.2
  101.8 1.5 %collective-permute-start.1 = (bf16[64,896]{1,0:T(8,128)(2,1)S(1)}, bf16[64,896]{1,0:T(8,128)(2,1)S(1)}, u32[]{:S(2)}, u32[]{:S(2)}) collective-permute-start(bf16[64,896]{1,0:T(8,128)(2,1)S(1)} %get-tuple-element.27), channel_id=1, source_target_pairs={{0,4},{1,5},{2,6},{3,7},{4,0},{5,1},{6,2},{7,3},{8,12},{9,13},{10,... | collective-permute-start | bytes 344072 | tf_op jit(solution)/shard_map/ppermute | solution.py:39
  103.3 0.0 copy-start
  103.3 16.0 %weight_grads.1 = (bf16[4,896,1024]{2,1,0:T(8,128)(2,1)}, bf16[4,896,1024]{2,1,0:T(8,128)(2,1)}, bf16[4,1024,896]{2,1,0:T(8,128)(2,1)}) custom-call(bf16[4,256,896]{2,1,0:T(8,128)(2,1)} %get-tuple-element.17.x_ref, bf16[4,256,896]{2,1,0:T(8,128)(2,1)} %get-tuple-element.18.dy_ref, bf16[4,256,1024]{2,1,0:T(8,128)(2,1)} %get-tuple-element.19.gate_ref, ...), custom_call_target="tpu_custom_call" | custom-call | flops 5637144576 | bytes 33554432 | tf_op jit(solution)/shard_map/weight_grads/pallas_call | solution.py:529
  119.3 0.0 collective-permute-done
  119.3 0.0 collective-permute-done.2
  119.3 0.0 collective-permute-done.1
  119.3 1.6 %fusion.2 = bf16[64,896]{1,0:T(8,128)(2,1)} fusion(bf16[64,896]{1,0:T(8,128)(2,1)S(1)} %collective-permute-done.2, bf16[64,896]{1,0:T(8,128)(2,1)S(1)} %collective-permute-done.1, bf16[64,896]{1,0:T(8,128)(2,1)S(1)} %collective-permute-done, bf16[4,64,896]{2,1,0:T(8,128)(2,1)} %get-tuple-element.16), kind=kLoop, calls=%fused_computation.3 | loop fusion | flops 458752 | bytes 573440 | tf_op jit(solution)/shard_map/convert_element_type | solution.py:47
  120.9 0.0 copy-done
  120.9 0.6 copy.13
Async XLA Ops:
  99.7 19.6 %collective-permute-start = (bf16[64,896]{1,0:T(8,128)(2,1)S(1)}, bf16[64,896]{1,0:T(8,128)(2,1)S(1)}, u32[]{:S(2)}, u32[]{:S(2)}) collective-permute-start(bf16[64,896]{1,0:T(8,128)(2,1)S(1)} %get-tuple-element.25), channel_id=1, source_target_pairs={{0,6},{1,7},{2,0},{3,1},{4,2},{5,3},{6,4},{7,5},{8,14},{9,15},{10,... | collective-permute-start | bytes 344072 | tf_op jit(solution)/shard_map/ppermute | solution.py:39
  101.2 18.1 %collective-permute-start.2 = (bf16[64,896]{1,0:T(8,128)(2,1)S(1)}, bf16[64,896]{1,0:T(8,128)(2,1)S(1)}, u32[]{:S(2)}, u32[]{:S(2)}) collective-permute-start(bf16[64,896]{1,0:T(8,128)(2,1)S(1)} %get-tuple-element.26), channel_id=1, source_target_pairs={{0,2},{1,3},{2,4},{3,5},{4,6},{5,7},{6,0},{7,1},{8,10},{9,11},{10,... | collective-permute-start | bytes 344072 | tf_op jit(solution)/shard_map/ppermute | solution.py:39
  101.8 17.5 %collective-permute-start.1 = (bf16[64,896]{1,0:T(8,128)(2,1)S(1)}, bf16[64,896]{1,0:T(8,128)(2,1)S(1)}, u32[]{:S(2)}, u32[]{:S(2)}) collective-permute-start(bf16[64,896]{1,0:T(8,128)(2,1)S(1)} %get-tuple-element.27), channel_id=1, source_target_pairs={{0,4},{1,5},{2,6},{3,7},{4,0},{5,1},{6,2},{7,3},{8,12},{9,13},{10,... | collective-permute-start | bytes 344072 | tf_op jit(solution)/shard_map/ppermute | solution.py:39
  103.3 17.6 %copy-start = (bf16[64,896]{1,0:T(8,128)(2,1)S(1)}, bf16[64,896]{1,0:T(8,128)(2,1)}, u32[]{:S(2)}) copy-start(bf16[64,896]{1,0:T(8,128)(2,1)} %get-tuple-element.33) | copy-start | bytes 344068
